TPU v7x, 32 devices: a whole 2x2x4 slice. The times are simulated.
32 devices in a mesh: band: 2 (over y), dom: 16 (over z, x, core).
Axes of the slice: x: 2, y: 2, z: 4, core: 2. Of those that a mesh axis runs over, the one named last changes fastest.
Arguments:
- orbitals: bfloat16 [512, 32, 32, 128], P('band', 'dom'), may hold values from -270 to 270
- potential: float32 [32, 32, 128], P('dom'), may hold values from 0 to 4
Outputs:
- rotated: bfloat16 [512, 32, 32, 128], P('band', 'dom')
All inputs are finite; a program needn't handle non-finite values.
Results may differ from a plain program's by a relative error of at most 0.025.
Values may be sent and summed in bfloat16 or wider, within the bound.
A program may use at most 128 MiB of HBM per device.

v0:
```python
from functools import partial

import jax
import jax.numpy as jnp
from jax import lax
from jax.sharding import PartitionSpec as P

spectrum_center = 7.5
spectrum_half = 4.5


def padded_2(cells, sides, width):
    for axis, dim in sides:
        count = lax.axis_size(axis)
        ends = count - 1
        head = lax.slice_in_dim(cells, 0, width, axis=dim)
        tail = lax.slice_in_dim(cells, cells.shape[dim] - width, cells.shape[dim], axis=dim)
        cells = jnp.concatenate(
            [
                lax.ppermute(tail, axis, [(i, (i + 1) % count) for i in range(ends)]),
                cells,
                lax.ppermute(head, axis, [((i + 1) % count, i) for i in range(ends)]),
            ],
            axis=dim,
        )
    return cells


def neighbours(padded, axis_dim, offset):
    index_list = [slice(None), slice(2, -2), slice(2, -2), slice(2, -2)]
    index_list[axis_dim] = slice(2 + offset, padded.shape[axis_dim] - 2 + offset)
    return padded[tuple(index_list)]


def hamiltonian(padded, potential):
    center = neighbours(padded, 1, 0)
    laplace = -7.5 * center
    for axis_dim in (1, 2, 3):
        near_sum = neighbours(padded, axis_dim, 1) + neighbours(padded, axis_dim, -1)
        far_sum = neighbours(padded, axis_dim, 2) + neighbours(padded, axis_dim, -2)
        laplace = laplace + 4.0 / 3.0 * near_sum - 1.0 / 12.0 * far_sum
    return (-0.5 * laplace + potential * center, center)


def chebyshev(field, operate):
    image, anchor = operate(field)
    degree_one = ((image - spectrum_center * anchor) / spectrum_half).astype(jnp.bfloat16)
    image, current = operate(degree_one)
    second = (2.0 * (image - spectrum_center * current) / spectrum_half - anchor).astype(
        jnp.bfloat16
    )
    image, latest = operate(second)
    return (2.0 * (image - spectrum_center * latest) / spectrum_half - current).astype(jnp.bfloat16)


def operator_on(field, potential):
    widened = padded_2(field, (("dom", 1),), 2)
    padded = jnp.pad(widened.astype(jnp.float32), ((0, 0), (0, 0), (2, 2), (2, 2)))
    return hamiltonian(padded, potential)


def rotation_from(gram):
    factor = jnp.linalg.cholesky(gram)
    identity = jnp.eye(gram.shape[0], dtype=jnp.float32)
    inverse_factor = lax.linalg.triangular_solve(factor, identity, left_side=True, lower=True)
    return inverse_factor.astype(jnp.bfloat16)


def local(orbitals, potential):
    orb_count = orbitals.shape[0]
    cells_dev = orbitals.shape[1] * orbitals.shape[2] * orbitals.shape[3]
    total_cells = cells_dev * lax.axis_size("dom")
    filtered = chebyshev(orbitals, partial(operator_on, potential=potential))
    flat = filtered.reshape(orb_count, cells_dev)
    contract = (((1,), (1,)), ((), ()))
    everyone = lax.all_gather(flat, "band", axis=0, tiled=True)
    row_terms = lax.dot_general(flat, everyone, contract, preferred_element_type=jnp.float32)
    summed = lax.psum(row_terms, "dom")
    gram = lax.all_gather(summed, "band", axis=0, tiled=True) / total_cells
    rotation = rotation_from(gram)
    own_rows = lax.dynamic_slice_in_dim(rotation, lax.axis_index("band") * orb_count, orb_count, 0)
    result = jnp.dot(own_rows, everyone, preferred_element_type=jnp.float32).astype(jnp.bfloat16)
    return result.reshape(orbitals.shape)


def solution(mesh):
    placed = (P("band", "dom", None, None), P("dom", None, None))
    return jax.shard_map(
        local, mesh=mesh, in_specs=placed, out_specs=P("band", "dom", None, None), check_vma=False
    )
```

profile of v0, /device:TPU:9, one launch (start us, length us, event | category | flops | bytes accessed | tf_op | source)
XLA Modules:
  0.0 845.9 jit_solution(3365407172377089460)
XLA Ops:
  6.5 3.8 collective-permute-start
  10.3 1.9 collective-permute-start.1
  12.3 88.8 %collective-permute-done = bf16[256,2,32,128]{3,2,1,0:T(8,128)(2,1)S(1)} collective-permute-done((bf16[256,2,32,128]{3,2,1,0:T(8,128)(2,1)}, bf16[256,2,32,128]{3,2,1,0:T(8,128)(2,1)S(1)}, u32[]{:S(2)}, u32[]{:S(2)}) %collective-permute-start) | collective-permute-done | bytes 4194336 | tf_op jit(solution)/shard_map/ppermute | solution.py:20
  102.5 10.2 %maximum_convert_fusion = f32[256,6,32,128]{3,2,1,0:T(8,128)} fusion(bf16[256,2,32,128]{3,2,1,0:T(8,128)(2,1)S(1)} %collective-permute-done.1, bf16[256,2,32,128]{3,2,1,0:T(8,128)(2,1)} %param.2, bf16[256,2,32,128]{3,2,1,0:T(8,128)(2,1)S(1)} %collective-permute-done), kind=kLoop, calls=%fused_computation.26 | loop fusion | flops 18874368 | bytes 37748736 | tf_op jit(solution)/shard_map/convert_element_type | solution.py:58
  112.7 41.4 %multiply_convert_fusion = bf16[256,2,32,128]{3,2,1,0:T(8,128)(2,1)} fusion(f32[256,6,32,128]{3,2,1,0:T(8,128)} %maximum_convert_fusion, f32[2,32,128]{2,1,0:T(8,128)S(1)} %copy-done), kind=kLoop, calls=%fused_computation.95 | loop fusion | flops 54525952 | bytes 71335936 | tf_op jit(solution)/shard_map/convert_element_type | solution.py:47
  154.1 2.8 collective-permute-start.2
  156.9 1.9 collective-permute-start.3
  158.8 88.8 %collective-permute-done.2 = bf16[256,2,32,128]{3,2,1,0:T(8,128)(2,1)S(1)} collective-permute-done((bf16[256,2,32,128]{3,2,1,0:T(8,128)(2,1)}, bf16[256,2,32,128]{3,2,1,0:T(8,128)(2,1)S(1)}, u32[]{:S(2)}, u32[]{:S(2)}) %collective-permute-start.2) | collective-permute-done | bytes 4194336 | tf_op jit(solution)/shard_map/ppermute | solution.py:20
  247.6 10.2 %maximum_convert_fusion.1 = f32[256,6,32,128]{3,2,1,0:T(8,128)} fusion(bf16[256,2,32,128]{3,2,1,0:T(8,128)(2,1)S(1)} %collective-permute-done.3, bf16[256,2,32,128]{3,2,1,0:T(8,128)(2,1)} %multiply_convert_fusion, bf16[256,2,32,128]{3,2,1,0:T(8,128)(2,1)S(1)} %collective-permute-done.2), kind=kLoop, calls=%fused_computation.27 | loop fusion | flops 18874368 | bytes 37748736 | tf_op jit(solution)/shard_map/convert_element_type | solution.py:58
  257.7 43.5 %subtract_convert_fusion.1 = bf16[256,2,32,128]{3,2,1,0:T(8,128)(2,1)} fusion(f32[256,6,32,128]{3,2,1,0:T(8,128)} %maximum_convert_fusion.1, f32[256,6,32,128]{3,2,1,0:T(8,128)} %maximum_convert_fusion, f32[2,32,128]{2,1,0:T(8,128)S(1)} %copy-done), kind=kLoop, calls=%fused_computation.94 | loop fusion | flops 56623104 | bytes 79724544 | tf_op jit(solution)/shard_map/convert_element_type | solution.py:49
  301.2 4.3 collective-permute-start.4
  305.5 2.1 collective-permute-start.5
  307.6 88.6 %collective-permute-done.4 = bf16[256,2,32,128]{3,2,1,0:T(8,128)(2,1)S(1)} collective-permute-done((bf16[256,2,32,128]{3,2,1,0:T(8,128)(2,1)}, bf16[256,2,32,128]{3,2,1,0:T(8,128)(2,1)S(1)}, u32[]{:S(2)}, u32[]{:S(2)}) %collective-permute-start.4) | collective-permute-done | bytes 4194336 | tf_op jit(solution)/shard_map/ppermute | solution.py:20
  396.2 10.2 %maximum_convert_fusion.2 = f32[256,6,32,128]{3,2,1,0:T(8,128)} fusion(bf16[256,2,32,128]{3,2,1,0:T(8,128)(2,1)S(1)} %collective-permute-done.5, bf16[256,2,32,128]{3,2,1,0:T(8,128)(2,1)} %subtract_convert_fusion.1, bf16[256,2,32,128]{3,2,1,0:T(8,128)(2,1)S(1)} %collective-permute-done.4), kind=kLoop, calls=%fused_computation.28 | loop fusion | flops 18874368 | bytes 37748736 | tf_op jit(solution)/shard_map/convert_element_type | solution.py:58
  406.4 43.9 %subtract_convert_fusion = bf16[256,2,32,128]{3,2,1,0:T(8,128)(2,1)} fusion(f32[256,6,32,128]{3,2,1,0:T(8,128)} %maximum_convert_fusion.2, f32[256,6,32,128]{3,2,1,0:T(8,128)} %maximum_convert_fusion.1, f32[2,32,128]{2,1,0:T(8,128)S(1)} %copy-done), kind=kLoop, calls=%fused_computation.93 | loop fusion | flops 56623104 | bytes 79724544 | tf_op jit(solution)/shard_map/convert_element_type | solution.py:53
  450.3 12.3 %copy.10 = bf16[32,8,64,128]{3,1,2,0:T(8,128)(2,1)} copy(bf16[32,8,64,128]{3,2,1,0:T(8,128)(2,1)} %bitcast.66) | data formatting | bytes 8388608
  462.7 103.9 %all-gather.3.cloned.1.call-done = bf16[512,8192]{1,0:T(8,128)(2,1)} async-done(((bf16[256,8192]{1,0:T(8,128)(2,1)}), bf16[512,8192]{1,0:T(8,128)(2,1)}) %all-gather.3.cloned.1.call-update) | async-done | bytes 8388624 | tf_op jit(solution)/shard_map/all_gather | solution.py:76
  566.5 9.0 %fusion.94 = f32[256,512]{0,1:T(8,128)} fusion(bf16[512,8192]{1,0:T(8,128)(2,1)} %all-gather.3.cloned.1.call-done, bf16[32,8,64,128]{3,2,1,0:T(8,128)(2,1)} %bitcast.67), kind=kOutput, calls=%fused_computation.173 | convolution fusion | flops 2147483648 | bytes 13107200 | tf_op jit(solution)/shard_map/dot_general | solution.py:77
  576.0 89.2 %all-reduce.6.cloned.1.call-done = f32[256,512]{0,1:T(8,128)} async-done(((f32[256,512]{0,1:T(8,128)}), f32[256,512]{0,1:T(8,128)}) %all-reduce.6.cloned.1.call-update) | async-done | bytes 524304 | tf_op jit(solution)/shard_map/psum | solution.py:78
  666.2 23.0 %all-gather.5.cloned.1.call-done = f32[512,512]{0,1:T(8,128)} async-done(((f32[256,512]{0,1:T(8,128)}), f32[512,512]{0,1:T(8,128)}) %all-gather.5.cloned.1.call-update) | async-done | bytes 1048592 | tf_op jit(solution)/shard_map/all_gather | solution.py:79
  692.3 11.7 %cholesky.104 = f32[128,128]{1,0:T(8,128)S(1)} custom-call(f32[128,128]{1,0:T(8,128)S(1)} %cholesky.266), custom_call_target="Cholesky" | custom-call | tf_op jit(solution)/shard_map/jit(cholesky)/cholesky | solution.py:63
  704.2 9.8 %custom-call.30 = f32[1,128,128]{1,2,0:T(8,128)S(1)} custom-call(f32[1,128,128]{2,1,0:T(8,128)S(1)} %get-tuple-element.32), custom_call_target="InvertDiagBlocksLowerTriangular" | custom-call | tf_op jit(solution)/shard_map/jit(cholesky)/cholesky | solution.py:63
  714.7 11.7 %cholesky.217 = f32[128,128]{1,0:T(8,128)S(1)} custom-call(f32[128,128]{1,0:T(8,128)S(1)} %cholesky.270), custom_call_target="Cholesky" | custom-call | tf_op jit(solution)/shard_map/jit(cholesky)/cholesky | solution.py:63
  726.4 10.0 %custom-call.31 = f32[1,128,128]{1,2,0:T(8,128)S(1)} custom-call(f32[1,128,128]{2,1,0:T(8,128)S(1)} %get-tuple-element.29), custom_call_target="InvertDiagBlocksLowerTriangular" | custom-call | tf_op jit(solution)/shard_map/jit(cholesky)/cholesky | solution.py:63
  737.1 11.7 %cholesky.238 = f32[128,128]{1,0:T(8,128)S(1)} custom-call(f32[128,128]{1,0:T(8,128)S(1)} %cholesky.275), custom_call_target="Cholesky" | custom-call | tf_op jit(solution)/shard_map/jit(cholesky)/cholesky | solution.py:63
  749.5 9.8 %custom-call.32 = f32[1,128,128]{1,2,0:T(8,128)S(1)} custom-call(f32[1,128,128]{2,1,0:T(8,128)S(1)} %get-tuple-element.26), custom_call_target="InvertDiagBlocksLowerTriangular" | custom-call | tf_op jit(solution)/shard_map/jit(cholesky)/cholesky | solution.py:63
  759.9 11.9 %cholesky.255 = f32[128,128]{1,0:T(8,128)S(1)} custom-call(f32[128,128]{1,0:T(8,128)S(1)} %convolution_subtract_fusion.5), custom_call_target="Cholesky" | custom-call | tf_op jit(solution)/shard_map/jit(cholesky)/cholesky | solution.py:63
  775.6 10.1 %while.1 = (s32[]{:T(128)}, f32[512,512]{1,0:T(8,128)S(1)}, s32[4,2]{0,1:T(2,128)S(1)}, f32[4,128,128]{2,1,0:T(8,128)}, s32[]{:T(128)}) while((s32[]{:T(128)}, f32[512,512]{1,0:T(8,128)S(1)}, s32[4,2]{0,1:T(2,128)S(1)}, f32[4,128,128]{2,1,0:T(8,128)}, s32[]{:T(128)}) %tuple.30), condition=%wide.while_cond, body=%wide.while_body.sunk | while | flops 2 | bytes 132705 | solution.py:65
  783.8 1.9 bitcast_dynamic-update-slice_fusion.2
  785.7 40.1 %custom-call.33 = f32[4,128,128]{1,2,0:T(8,128)S(1)} custom-call(f32[4,128,128]{2,1,0:T(8,128)} %get-tuple-element.12), custom_call_target="InvertDiagBlocksLowerTriangular" | custom-call | tf_op jit(solution)/shard_map/triangular_solve | solution.py:65
  829.7 6.2 fusion.57
  835.9 3.2 copy.7
  (55 shorter events, 22.2 us)
Async XLA Ops:
  6.5 106.1 %copy-start = (f32[2,32,128]{2,1,0:T(8,128)S(1)}, f32[2,32,128]{2,1,0:T(8,128)}, u32[]{:S(2)}) copy-start(f32[2,32,128]{2,1,0:T(8,128)} %param.3) | copy-start | bytes 98308
  6.5 560.0 %all-gather.3.cloned.1.call-start = ((), (), s32[]{:S(2)}) async-start(), calls=%async_computation | async-start | bytes 12582912 | tf_op jit(solution)/shard_map/all_gather | solution.py:76
  6.5 94.5 %collective-permute-start = (bf16[256,2,32,128]{3,2,1,0:T(8,128)(2,1)}, bf16[256,2,32,128]{3,2,1,0:T(8,128)(2,1)S(1)}, u32[]{:S(2)}, u32[]{:S(2)}) collective-permute-start(bf16[256,2,32,128]{3,2,1,0:T(8,128)(2,1)} %param.2), channel_id=1, source_target_pairs={{0,1},{1,2},{2,3},{3,4},{4,5},{5,6},{6,7},{7,8},{8,9},{9,10},{10,1... | collective-permute-start | bytes 12582920 | tf_op jit(solution)/shard_map/ppermute | solution.py:20
  10.3 92.2 %collective-permute-start.1 = (bf16[256,2,32,128]{3,2,1,0:T(8,128)(2,1)}, bf16[256,2,32,128]{3,2,1,0:T(8,128)(2,1)S(1)}, u32[]{:S(2)}, u32[]{:S(2)}) collective-permute-start(bf16[256,2,32,128]{3,2,1,0:T(8,128)(2,1)} %param.2), channel_id=1, source_target_pairs={{1,0},{2,1},{3,2},{4,3},{5,4},{6,5},{7,6},{8,7},{9,8},{10,9},{11,1... | collective-permute-start | bytes 12582920 | tf_op jit(solution)/shard_map/ppermute | solution.py:22
  154.1 93.5 %collective-permute-start.2 = (bf16[256,2,32,128]{3,2,1,0:T(8,128)(2,1)}, bf16[256,2,32,128]{3,2,1,0:T(8,128)(2,1)S(1)}, u32[]{:S(2)}, u32[]{:S(2)}) collective-permute-start(bf16[256,2,32,128]{3,2,1,0:T(8,128)(2,1)} %multiply_convert_fusion), channel_id=1, source_target_pairs={{0,1},{1,2},{2,3},{3,4},{4,5},{5,6},{6,7},{7,8},{8,9},{9,10},{10,1... | collective-permute-start | bytes 12582920 | tf_op jit(solution)/shard_map/ppermute | solution.py:20
  156.9 90.7 %collective-permute-start.3 = (bf16[256,2,32,128]{3,2,1,0:T(8,128)(2,1)}, bf16[256,2,32,128]{3,2,1,0:T(8,128)(2,1)S(1)}, u32[]{:S(2)}, u32[]{:S(2)}) collective-permute-start(bf16[256,2,32,128]{3,2,1,0:T(8,128)(2,1)} %multiply_convert_fusion), channel_id=1, source_target_pairs={{1,0},{2,1},{3,2},{4,3},{5,4},{6,5},{7,6},{8,7},{9,8},{10,9},{11,1... | collective-permute-start | bytes 12582920 | tf_op jit(solution)/shard_map/ppermute | solution.py:22
  301.2 95.0 %collective-permute-start.4 = (bf16[256,2,32,128]{3,2,1,0:T(8,128)(2,1)}, bf16[256,2,32,128]{3,2,1,0:T(8,128)(2,1)S(1)}, u32[]{:S(2)}, u32[]{:S(2)}) collective-permute-start(bf16[256,2,32,128]{3,2,1,0:T(8,128)(2,1)} %subtract_convert_fusion.1), channel_id=1, source_target_pairs={{0,1},{1,2},{2,3},{3,4},{4,5},{5,6},{6,7},{7,8},{8,9},{9,10},{10,1... | collective-permute-start | bytes 12582920 | tf_op jit(solution)/shard_map/ppermute | solution.py:20
  305.5 90.7 %collective-permute-start.5 = (bf16[256,2,32,128]{3,2,1,0:T(8,128)(2,1)}, bf16[256,2,32,128]{3,2,1,0:T(8,128)(2,1)S(1)}, u32[]{:S(2)}, u32[]{:S(2)}) collective-permute-start(bf16[256,2,32,128]{3,2,1,0:T(8,128)(2,1)} %subtract_convert_fusion.1), channel_id=1, source_target_pairs={{1,0},{2,1},{3,2},{4,3},{5,4},{6,5},{7,6},{8,7},{9,8},{10,9},{11,1... | collective-permute-start | bytes 12582920 | tf_op jit(solution)/shard_map/ppermute | solution.py:22
  462.6 202.6 %all-reduce.6.cloned.1.call-start = ((), (), s32[]{:S(2)}) async-start(), calls=%async_computation.1 | async-start | bytes 1048576 | tf_op jit(solution)/shard_map/psum | solution.py:78
  575.5 113.6 %all-gather.5.cloned.1.call-start = ((), (), s32[]{:S(2)}) async-start(), calls=%async_computation.2 | async-start | bytes 1572864 | tf_op jit(solution)/shard_map/all_gather | solution.py:79
Sparse Core Ops, SparseCore 0:
  462.8 103.7 all-gather.2
  575.6 89.5 all-reduce.5
  666.8 22.3 all-gather.4
where the time goes:
time: 854 us; the launch traced here: 846 us
  waiting for transfers between devices  484 us (57%)
  other arithmetic  282 us (33%)
  local copies, waits for them, and re-layouts  26.1 us (3%)
  matrix products  20.8 us (2%)
  starting transfers between devices  17.3 us (2%)
  between operations  16 us (2%)
    ppermute x3, waiting for transfers between devices, padded_2(): lax.ppermute(tail, axis, [(i, (i + 1) % count) for i in range(ends)])  266 us
    all_gather x1, waiting for transfers between devices, local(): everyone = lax.all_gather(flat, 'band', axis=0, tiled=True)  104 us
    psum x1, waiting for transfers between devices, local(): summed = lax.psum(row_terms, 'dom')  89.2 us
    another operation x14, other arithmetic, rotation_from(): factor = jnp.linalg.cholesky(gram)  78.7 us
    convert_element_type x1, other arithmetic, chebyshev(): (2.0 * (image - spectrum_center * latest) / spectrum_half - current).asty...  43.9 us
    convert_element_type x1, other arithmetic, chebyshev(): (2.0 * (image - spectrum_center * current) / spectrum_half - anchor).asty...  43.5 us
    convert_element_type x1, other arithmetic, chebyshev(): ((image - spectrum_center * anchor) / spectrum_half).astype(jnp.bfloat16)  41.4 us
    another operation x3, other arithmetic, rotation_from(): lax.linalg.triangular_solve(factor, identity, left_side=True, lower=True)  40.3 us
  transfers between devices with their start and end apart: 9, of which 7 were waited for; matrix products, arithmetic and copies ran while one was open for 0% of the time, Pallas kernels for 0%

commit v1 on v0

v1 whole, which is shorter than its diff:
```python
import functools

import jax
import jax.numpy as jnp
import numpy as np
from jax import lax
from jax.experimental import pallas as pl
from jax.experimental.pallas import tpu as pltpu
from jax.sharding import PartitionSpec as P

MESH = pl.DeviceIdType.MESH
spectrum_center = 7.5
spectrum_half = 4.5
GROUP = 4
CHUNK = 16


def band_matrix(blocks, size):
    one = 16.0 * (np.eye(size, k=1) + np.eye(size, k=-1)) - np.eye(size, k=2) - np.eye(size, k=-2)
    return jnp.asarray(np.kron(np.eye(blocks), one), jnp.bfloat16)


def filter_kernel(
    bands, doms, orb_ref, pot_ref, ty_ref, tz_ref, gram_ref, held_ref,
    f0, f1, f2, pot, wide, sent, held,
    in_send, in_recv, pot_send, pot_recv, halo_send, halo_recv, out_send, out_recv, own_sem,
):
    orbs, planes, ny, nz = orb_ref.shape
    share = orbs // GROUP
    slab = GROUP * planes
    chunks = share // CHUNK
    rows_dev = planes * ny
    rows_part = rows_dev // bands
    b, d = lax.axis_index("band"), lax.axis_index("dom")
    g, z = lax.rem(d, GROUP), d // GROUP
    z_count = doms // GROUP
    base = z * GROUP
    has_low, has_high = z > 0, z < z_count - 1

    def peer(k, j=0):
        return (lax.rem(b + j, bands), base + lax.rem(g + k, GROUP))

    barrier = pltpu.get_barrier_semaphore()
    for k in range(GROUP):
        for j in range(bands):
            if k or j:
                pl.semaphore_signal(barrier, inc=1, device_id=peer(k, j), device_id_type=MESH)

    @pl.when(has_low)
    def _():
        pl.semaphore_signal(barrier, inc=1, device_id=(b, d - GROUP), device_id_type=MESH)

    @pl.when(has_high)
    def _():
        pl.semaphore_signal(barrier, inc=1, device_id=(b, d + GROUP), device_id_type=MESH)

    ends = jnp.where(has_low, 1, 0) + jnp.where(has_high, 1, 0)
    pl.semaphore_wait(barrier, GROUP * bands - 1 + ends)

    pot_copies, in_copies = [], {}
    own_planes = pl.ds(g * planes, planes)
    for k in range(1, GROUP):
        copy = pltpu.make_async_remote_copy(
            pot_ref, pot.at[own_planes], pot_send.at[k - 1], pot_recv.at[k - 1],
            device_id=peer(k), device_id_type=MESH,
        )
        copy.start()
        pot_copies.append(copy)
    own_pot = pltpu.make_async_copy(pot_ref, pot.at[own_planes], own_sem.at[chunks])
    own_pot.start()
    own_in = []
    for c in range(chunks):
        span = pl.ds(c * CHUNK, CHUNK)
        landing = f0.at[span, pl.ds(2 + g * planes, planes)]
        for k in range(1, GROUP):
            first = lax.rem(g + k, GROUP) * share + c * CHUNK
            copy = pltpu.make_async_remote_copy(
                orb_ref.at[pl.ds(first, CHUNK)], landing,
                in_send.at[c, k - 1], in_recv.at[c, k - 1],
                device_id=peer(k), device_id_type=MESH,
            )
            copy.start()
            in_copies[c, k] = copy
        copy = pltpu.make_async_copy(
            orb_ref.at[pl.ds(g * share + c * CHUNK, CHUNK)], landing, own_sem.at[c]
        )
        copy.start()
        own_in.append(copy)

    fields = (f0, f1, f2)

    @pl.when(jnp.logical_not(has_low))
    def _():
        for field in fields:
            field[:, 0:2] = jnp.zeros((share, 2, ny, nz), jnp.bfloat16)

    @pl.when(jnp.logical_not(has_high))
    def _():
        for field in fields:
            field[:, slab + 2 :] = jnp.zeros((share, 2, ny, nz), jnp.bfloat16)

    def halo(s, c):
        field, span = fields[s], pl.ds(c * CHUNK, CHUNK)
        down = pltpu.make_async_remote_copy(
            field.at[span, pl.ds(2, 2)], field.at[span, pl.ds(slab + 2, 2)],
            halo_send.at[s, c, 0], halo_recv.at[s, c, 0],
            device_id=(b, d - GROUP), device_id_type=MESH,
        )
        up = pltpu.make_async_remote_copy(
            field.at[span, pl.ds(slab, 2)], field.at[span, pl.ds(0, 2)],
            halo_send.at[s, c, 1], halo_recv.at[s, c, 1],
            device_id=(b, d + GROUP), device_id_type=MESH,
        )
        return down, up

    def send_halo(s, c):
        down, up = halo(s, c)
        pl.when(has_low)(down.start)
        pl.when(has_high)(up.start)

    def wait_halo(s, c):
        down, up = halo(s, c)
        pl.when(has_low)(up.wait_recv)
        pl.when(has_high)(down.wait_recv)

    def wait_halo_sent(s, c):
        down, up = halo(s, c)
        pl.when(has_low)(down.wait_send)
        pl.when(has_high)(up.wait_send)

    def apply(s, c):
        field = fields[s]
        factor = (1.0 if s == 0 else 2.0) / spectrum_half
        shift = 0.5 * 7.5 - spectrum_center

        def value(p, first):
            span = pl.ds(first, 8)

            def at(q):
                return field[span, q].reshape(8 * ny, nz)

            def wide_at(q):
                return at(q).astype(jnp.float32)

            v = at(p + 2)
            total = jnp.dot(ty_ref[...], v, preferred_element_type=jnp.float32)
            total += jnp.dot(v, tz_ref[...], preferred_element_type=jnp.float32)
            total += 16.0 * (wide_at(p + 1) + wide_at(p + 3)) - (wide_at(p) + wide_at(p + 4))
            scale = (pot[p] + shift) * factor
            own = (v.astype(jnp.float32).reshape(8, ny, nz) * scale[None]).reshape(8 * ny, nz)
            new = own - total * (factor / 24.0)
            if s > 0:
                old = fields[s - 1][span, p + 2].reshape(8 * ny, nz)
                new = new - old.astype(jnp.float32)
            return new

        if s < 2:
            def body(i, _):
                p, first = i // 2, pl.multiple_of(c * CHUNK + lax.rem(i, 2) * 8, 8)
                new = value(p, first).astype(jnp.bfloat16)
                fields[s + 1][pl.ds(first, 8), p + 2] = new.reshape(8, ny, nz)
                return 0

            lax.fori_loop(0, 2 * slab, body, 0)
        else:
            def body(p, _):
                for h in range(2):
                    wide[pl.ds(h * 8 * ny, 8 * ny), :] = value(p, c * CHUNK + h * 8)
                for y in range(ny):
                    rows = wide[pl.ds(y, CHUNK, stride=ny), :]
                    sent[c, p * ny + y] = rows.astype(jnp.bfloat16)
                return 0

            lax.fori_loop(0, slab, body, 0)

    own_out, out_copies = [], []

    def send_out(c):
        landing = held.at[(b * GROUP + g) * chunks + c]
        for k in range(GROUP):
            for j in range(bands):
                row = lax.rem(g + k, GROUP) * rows_dev + lax.rem(b + j, bands) * rows_part
                source = sent.at[c, pl.ds(row, rows_part)]
                if k or j:
                    at = k * bands + j - 1
                    copy = pltpu.make_async_remote_copy(
                        source, landing, out_send.at[c, at], out_recv.at[c, at],
                        device_id=peer(k, j), device_id_type=MESH,
                    )
                    out_copies.append(copy)
                else:
                    copy = pltpu.make_async_copy(source, landing, own_sem.at[chunks + 1 + c])
                    own_out.append(copy)
                copy.start()

    for copy in pot_copies:
        copy.wait_recv()
    own_pot.wait()
    for t in range(chunks + 3):
        if t < chunks:
            own_in[t].wait()
            for k in range(1, GROUP):
                in_copies[t, k].wait_recv()
            send_halo(0, t)
        for s in (2, 1, 0):
            c = t - 1 - s
            if 0 <= c < chunks:
                wait_halo(s, c)
                apply(s, c)
                if s < 2:
                    send_halo(s + 1, c)
                else:
                    send_out(c)

    for copy in own_out:
        copy.wait()
    for copy in out_copies:
        copy.wait_recv()
    keep = pltpu.make_async_copy(held, held_ref, own_sem.at[2 * chunks + 1])
    keep.start()

    everyone = bands * orbs
    step = min(8, rows_part)

    def terms(i, _):
        x = jnp.concatenate(
            [held[:, i * step + j].reshape(everyone, nz) for j in range(step)], axis=1
        )
        part = lax.dot_general(
            x, x, (((1,), (1,)), ((), ())), preferred_element_type=jnp.float32
        )
        gram_ref[...] += part
        return 0

    gram_ref[...] = jnp.zeros(gram_ref.shape, jnp.float32)
    lax.fori_loop(0, rows_part // step, terms, 0)

    for copy in pot_copies:
        copy.wait_send()
    for copy in in_copies.values():
        copy.wait_send()
    for s in range(3):
        for c in range(chunks):
            wait_halo_sent(s, c)
    for copy in out_copies:
        copy.wait_send()
    keep.wait()


def filter_and_gram(orbitals, potential, bands, doms):
    orbs, planes, ny, nz = orbitals.shape
    share, slab = orbs // GROUP, GROUP * planes
    chunks = share // CHUNK
    rows_part = planes * ny // bands
    held = (bands * orbs // CHUNK, rows_part, CHUNK, nz)
    field = pltpu.VMEM((share, slab + 4, ny, nz), jnp.bfloat16)
    others = GROUP * bands - 1
    dma = pltpu.SemaphoreType.DMA
    vmem = pl.BlockSpec(memory_space=pltpu.VMEM)
    hbm = pl.BlockSpec(memory_space=pl.ANY)
    return pl.pallas_call(
        functools.partial(filter_kernel, bands, doms),
        out_shape=(
            jax.ShapeDtypeStruct((bands * orbs, bands * orbs), jnp.float32),
            jax.ShapeDtypeStruct(held, jnp.bfloat16),
        ),
        in_specs=[hbm, vmem, vmem, vmem],
        out_specs=(vmem, hbm),
        scratch_shapes=[
            field, field, field,
            pltpu.VMEM((slab, ny, nz), jnp.float32),
            pltpu.VMEM((CHUNK * ny, nz), jnp.float32),
            pltpu.VMEM((chunks, slab * ny, CHUNK, nz), jnp.bfloat16),
            pltpu.VMEM(held, jnp.bfloat16),
            dma((chunks, GROUP - 1)), dma((chunks, GROUP - 1)),
            dma((GROUP - 1,)), dma((GROUP - 1,)),
            dma((3, chunks, 2)), dma((3, chunks, 2)),
            dma((chunks, others)), dma((chunks, others)),
            dma((2 * chunks + 2,)),
        ],
        compiler_params=pltpu.CompilerParams(
            collective_id=0, has_side_effects=True, vmem_limit_bytes=56 * 2**20
        ),
        name="filter_and_gram",
    )(orbitals, potential, band_matrix(8, ny), band_matrix(1, nz))


def rotate_kernel(own_ref, *refs):
    pieces, (first_ref, out_ref, wide) = refs[:-3], refs[-3:]
    count, rows, chunk, nz = pieces[0].shape
    orbs, all_rows = out_ref.shape[0], out_ref.shape[1]
    for j, piece in enumerate(pieces):
        start = first_ref[j]

        def body(i, _, piece=piece, start=start):
            x = jnp.concatenate(
                [piece[:, 2 * i + h].reshape(count * chunk, nz) for h in range(2)], axis=1
            )
            y = jnp.dot(own_ref[...], x, preferred_element_type=jnp.float32)
            for h in range(2):
                at = pl.ds(start + 2 * i + h, orbs, stride=all_rows)
                wide[at, :] = y[:, h * nz : (h + 1) * nz]
            return 0

        lax.fori_loop(0, rows // 2, body, 0)

    def narrow(i, _):
        part = wide[pl.ds(pl.multiple_of(i * 8 * all_rows, 8 * all_rows), 8 * all_rows), :]
        out_ref[pl.ds(i * 8, 8)] = part.reshape(8, all_rows, nz).astype(jnp.bfloat16)
        return 0

    lax.fori_loop(0, orbs // 8, narrow, 0)


def rotate(own_rows, pieces, firsts, all_rows):
    orbs = own_rows.shape[0]
    nz = pieces[0].shape[3]
    vmem = pl.BlockSpec(memory_space=pltpu.VMEM)
    return pl.pallas_call(
        rotate_kernel,
        out_shape=jax.ShapeDtypeStruct((orbs, all_rows, nz), jnp.bfloat16),
        in_specs=[vmem] * (1 + len(pieces)) + [pl.BlockSpec(memory_space=pltpu.SMEM)],
        out_specs=vmem,
        scratch_shapes=[pltpu.VMEM((orbs * all_rows, nz), jnp.float32)],
        compiler_params=pltpu.CompilerParams(vmem_limit_bytes=48 * 2**20),
        name="rotate",
    )(own_rows, *pieces, firsts)


def rotation_from(gram):
    factor = jnp.linalg.cholesky(gram)
    identity = jnp.eye(gram.shape[0], dtype=jnp.float32)
    inverse_factor = lax.linalg.triangular_solve(factor, identity, left_side=True, lower=True)
    return inverse_factor.astype(jnp.bfloat16)


def local(bands, doms, orbitals, potential):
    orbs, planes, ny, nz = orbitals.shape
    all_rows = planes * ny
    total_cells = all_rows * nz * doms
    part, held = filter_and_gram(orbitals, potential, bands, doms)
    pieces = [held]
    for j in range(1, bands):
        ring = [((i + j) % bands, i) for i in range(bands)]
        pieces.append(lax.ppermute(held, "band", ring))
    gram = lax.psum(part, ("band", "dom")) / total_cells
    rotation = rotation_from(gram)
    b = lax.axis_index("band")
    own_rows = lax.dynamic_slice_in_dim(rotation, b * orbs, orbs, 0)
    firsts = (b + jnp.arange(bands, dtype=jnp.int32)) % bands * (all_rows // bands)
    result = rotate(own_rows, pieces, firsts.astype(jnp.int32), all_rows)
    return result.reshape(orbitals.shape)


def solution(mesh):
    placed = (P("band", "dom", None, None), P("dom", None, None))
    return jax.shard_map(
        functools.partial(local, mesh.shape["band"], mesh.shape["dom"]),
        mesh=mesh, in_specs=placed, out_specs=P("band", "dom", None, None), check_vma=False,
    )
```

time: 854 us -> 423 us (0.50)
  waiting for transfers between devices: 484 us -> 125 us
  other arithmetic: 282 us -> 123 us
  Pallas kernels: 0 us -> 131 us
  starting transfers between devices: 17.3 us -> 0.89 us
  matrix products: 20.8 us -> 5.81 us
  local copies, waits for them, and re-layouts: 26.1 us -> 13.5 us
    ppermute x6 -> x1, waiting for transfers between devices: 268 us -> 0.01 us  [local(): pieces.append(lax.ppermute(held, 'band', ring))]
    convert_element_type x6 -> x0, other arithmetic: 159 us -> none  [the longest x1 43.9 us: chebyshev(): (2.0 * (image - spectrum_center * latest) / spectrum_half - current).asty...]
    pallas_call x0 -> x2, Pallas kernels: none -> 131 us  [the longest x1 115 us: filter_and_gram(): pl.pallas_call(functools.partial(filter_kernel, bands, doms), out_shape=(...]
    all_gather x2 -> x0, waiting for transfers between devices: 127 us -> none  [the longest x1 104 us: local(): everyone = lax.all_gather(flat, 'band', axis=0, tiled=True)]
    psum x1, waiting for transfers between devices: 89.2 us -> 125 us  [local(): gram = lax.psum(part, ('band', 'dom')) / total_cells]
    ppermute x6 -> x1, starting transfers between devices: 16.8 us -> 0.89 us  [local(): pieces.append(lax.ppermute(held, 'band', ring))]
    unnamed x4 -> x6, local copies, waits for them, and re-layouts: 15.5 us -> 0.01 us
    dot_general x2 -> x0, matrix products: 15.2 us -> none  [the longest x1 8.96 us: local(): lax.dot_general(flat, everyone, contract, preferred_element_type=jnp.floa...]
  transfers between devices with their start and end apart: 9 -> 2, of which waited for: 7 -> 1; matrix products, arithmetic and copies ran while one was open for 0% -> 34% of each run, Pallas kernels for 0% -> 0%
where the time goes in v1:
time: 423 us; the launch traced here: 415 us
  Pallas kernels  131 us (31%)
  waiting for transfers between devices  125 us (30%)
  other arithmetic  123 us (29%)
  between operations  16.5 us (4%)
  local copies, waits for them, and re-layouts  13.5 us (3%)
  matrix products  5.81 us (1%)
    psum x1, waiting for transfers between devices, local(): gram = lax.psum(part, ('band', 'dom')) / total_cells  125 us
    pallas_call x1, Pallas kernels, filter_and_gram(): pl.pallas_call(functools.partial(filter_kernel, bands, doms), out_shape=(...  115 us
    another operation x14, other arithmetic, rotation_from(): factor = jnp.linalg.cholesky(gram)  78.7 us
    another operation x4, other arithmetic, rotation_from(): lax.linalg.triangular_solve(factor, identity, left_side=True, lower=True)  41 us
    pallas_call x1, Pallas kernels, rotate(): pl.pallas_call(rotate_kernel, out_shape=jax.ShapeDtypeStruct((orbs, all_r...  15.9 us
    another operation x12, local copies, waits for them, and re-layouts  10.5 us
  transfers between devices with their start and end apart: 2, of which 1 were waited for; matrix products, arithmetic and copies ran while one was open for 34% of the time, Pallas kernels for 0%

profile of v1, /device:TPU:9, one launch (start us, length us, event | category | flops | bytes accessed | tf_op | source)
XLA Modules:
  0.0 415.2 jit_solution(16535169466112448109)
XLA Ops:
  6.5 114.8 %filter_and_gram.1 = (f32[512,512]{1,0:T(8,128)}, bf16[32,32,16,128]{3,2,1,0:T(8,128)(2,1)}) custom-call(bf16[256,2,32,128]{3,2,1,0:T(8,128)(2,1)} %orb_ref.1, f32[2,32,128]{2,1,0:T(8,128)} %pot_ref.1, bf16[256,256]{1,0:T(8,128)(2,1)} %constant.176.clone.ty_ref, bf16[128,128]{1,0:T(8,128)(2,1)} %constant.177.clone.tz_ref), custom_call_target="tpu_custom_call" | custom-call | tf_op jit(solution)/shard_map/filter_and_gram/pallas_call | solution.py:261
  121.3 2.5 copy.5
  123.9 0.9 collective-permute-start
  124.8 0.8 iota_compare_fusion
  125.6 1.2 fusion.9
  126.8 124.5 %all-reduce.3.cloned.1.call-done = f32[512,512]{0,1:T(8,128)} async-done(((f32[512,512]{0,1:T(8,128)}), f32[512,512]{0,1:T(8,128)}) %all-reduce.3.cloned.1.call-update) | async-done | bytes 1048592 | tf_op jit(solution)/shard_map/psum | solution.py:346
  251.3 1.4 broadcast_multiply_fusion
  253.3 11.7 %cholesky.104 = f32[128,128]{1,0:T(8,128)S(1)} custom-call(f32[128,128]{1,0:T(8,128)S(1)} %cholesky.266), custom_call_target="Cholesky" | custom-call | tf_op jit(solution)/shard_map/jit(cholesky)/cholesky | solution.py:331
  265.0 9.8 %custom-call.30 = f32[1,128,128]{1,2,0:T(8,128)S(1)} custom-call(f32[1,128,128]{2,1,0:T(8,128)S(1)} %get-tuple-element.36), custom_call_target="InvertDiagBlocksLowerTriangular" | custom-call | tf_op jit(solution)/shard_map/jit(cholesky)/cholesky | solution.py:331
  275.7 11.7 %cholesky.217 = f32[128,128]{1,0:T(8,128)S(1)} custom-call(f32[128,128]{1,0:T(8,128)S(1)} %cholesky.270), custom_call_target="Cholesky" | custom-call | tf_op jit(solution)/shard_map/jit(cholesky)/cholesky | solution.py:331
  287.4 9.9 %custom-call.31 = f32[1,128,128]{1,2,0:T(8,128)S(1)} custom-call(f32[1,128,128]{2,1,0:T(8,128)S(1)} %get-tuple-element.33), custom_call_target="InvertDiagBlocksLowerTriangular" | custom-call | tf_op jit(solution)/shard_map/jit(cholesky)/cholesky | solution.py:331
  298.0 11.7 %cholesky.238 = f32[128,128]{1,0:T(8,128)S(1)} custom-call(f32[128,128]{1,0:T(8,128)S(1)} %cholesky.275), custom_call_target="Cholesky" | custom-call | tf_op jit(solution)/shard_map/jit(cholesky)/cholesky | solution.py:331
  309.8 9.8 %custom-call.32 = f32[1,128,128]{1,2,0:T(8,128)S(1)} custom-call(f32[1,128,128]{2,1,0:T(8,128)S(1)} %get-tuple-element.30), custom_call_target="InvertDiagBlocksLowerTriangular" | custom-call | tf_op jit(solution)/shard_map/jit(cholesky)/cholesky | solution.py:331
  320.2 11.9 %cholesky.255 = f32[128,128]{1,0:T(8,128)S(1)} custom-call(f32[128,128]{1,0:T(8,128)S(1)} %convolution_subtract_fusion.5), custom_call_target="Cholesky" | custom-call | tf_op jit(solution)/shard_map/jit(cholesky)/cholesky | solution.py:331
  332.1 0.7 compare_reduce_fusion.2
  334.1 0.6 compare_reduce_fusion.1
  335.4 0.6 compare_reduce_fusion
  336.8 10.5 %while.1 = (s32[]{:T(128)}, f32[512,512]{1,0:T(8,128)S(1)}, s32[4,2]{0,1:T(2,128)S(1)}, f32[4,128,128]{2,1,0:T(8,128)}, s32[]{:T(128)}) while((s32[]{:T(128)}, f32[512,512]{1,0:T(8,128)S(1)}, s32[4,2]{0,1:T(2,128)S(1)}, f32[4,128,128]{2,1,0:T(8,128)}, s32[]{:T(128)}) %tuple.30), condition=%wide.while_cond, body=%wide.while_body.sunk | while | flops 2 | bytes 132205 | solution.py:333
  336.9 0.6 fusion.45
  337.5 2.0 bitcast_dynamic-update-slice_fusion.2
  339.6 0.6 fusion.45
  340.1 2.0 bitcast_dynamic-update-slice_fusion.2
  342.2 0.6 fusion.45
  342.7 2.0 bitcast_dynamic-update-slice_fusion.2
  344.8 0.6 fusion.45
  345.4 2.0 bitcast_dynamic-update-slice_fusion.2
  347.4 40.1 %custom-call.33 = f32[4,128,128]{1,2,0:T(8,128)S(1)} custom-call(f32[4,128,128]{2,1,0:T(8,128)} %get-tuple-element.16), custom_call_target="InvertDiagBlocksLowerTriangular" | custom-call | tf_op jit(solution)/shard_map/triangular_solve | solution.py:333
  387.5 1.2 fusion.36
  389.6 0.4 convolution_subtract_fusion
  390.4 0.6 convolution_subtract_fusion.2
  391.5 0.7 fusion.12.own_ref
  392.2 15.9 %rotate.1 = bf16[256,64,128]{2,1,0:T(8,128)(2,1)} custom-call(bf16[256,512]{1,0:T(8,128)(2,1)S(1)} %fusion.12.own_ref, bf16[32,32,16,128]{3,2,1,0:T(8,128)(2,1)S(1)} %copy-done, bf16[32,32,16,128]{3,2,1,0:T(8,128)(2,1)} %collective-permute-done.refs_1_, s32[2]{0:T(128)S(1)} %fusion.31.refs_2_), custom_call_target="tpu_custom_call" | custom-call | tf_op jit(solution)/shard_map/rotate/pallas_call | solution.py:319
  (38 shorter events, 4.8 us)
Async XLA Ops:
  6.5 244.7 %all-reduce.3.cloned.1.call-start = ((), (), s32[]{:S(2)}) async-start(), calls=%async_computation | async-start | bytes 2097152 | tf_op jit(solution)/shard_map/psum | solution.py:346
  123.9 268.3 %collective-permute-start = (bf16[32,32,16,128]{3,2,1,0:T(8,128)(2,1)}, bf16[32,32,16,128]{3,2,1,0:T(8,128)(2,1)}, u32[]{:S(2)}, u32[]{:S(2)}) collective-permute-start(bf16[32,32,16,128]{3,2,1,0:T(8,128)(2,1)} %get-tuple-element.8.refs_0_), channel_id=1, source_target_pairs={{16,0},{0,16},{17,1},{1,17},{18,2},{2,18},{19,3},{3,19},{20,4},{4,... | collective-permute-start | bytes 12582920 | tf_op jit(solution)/shard_map/ppermute | solution.py:345
  251.3 1.8 copy-start.1
  253.3 135.5 %copy-start.2 = (f32[512,512]{1,0:T(8,128)S(1)}, f32[512,512]{1,0:T(8,128)}, u32[]{:S(2)}) copy-start(f32[512,512]{1,0:T(8,128)} %fusion.9) | copy-start | bytes 3145732
  387.5 4.7 %copy-start = (bf16[32,32,16,128]{3,2,1,0:T(8,128)(2,1)S(1)}, bf16[32,32,16,128]{3,2,1,0:T(8,128)(2,1)}, u32[]{:S(2)}) copy-start(bf16[32,32,16,128]{3,2,1,0:T(8,128)(2,1)} %get-tuple-element.8.refs_0_) | copy-start | bytes 12582916
Sparse Core Ops, SparseCore 0:
  124.0 127.2 all-reduce.2

commit v2 on v1

--- a/solution.py
+++ b/solution.py
@@ -327,11 +327,170 @@
     )(own_rows, *pieces, firsts)
 
 
+def sum_kernel(bands, doms, scale, part_ref, out_ref, near, far, whole, *sems):
+    near_send, near_recv, far_send, far_recv, all_send, all_recv = sems
+    size = part_ref.shape[0]
+    members = GROUP * bands
+    rows = size // members
+    z_count = doms // GROUP
+    b, d = lax.axis_index("band"), lax.axis_index("dom")
+    g, z = lax.rem(d, GROUP), d // GROUP
+    others = [(k, j) for k in range(GROUP) for j in range(bands) if k or j]
+
+    def place(k, j):
+        return lax.rem(g + k, GROUP), lax.rem(b + j, bands)
+
+    def near_device(k, j):
+        to_g, to_b = place(k, j)
+        return (to_b, z * GROUP + to_g)
+
+    def far_device(h):
+        return (b, lax.rem(z + h, z_count) * GROUP + g)
+
+    def block(to_g, to_b):
+        return pl.ds(pl.multiple_of((to_g * bands + to_b) * rows, rows), rows)
+
+    barrier = pltpu.get_barrier_semaphore()
+    for k, j in others:
+        pl.semaphore_signal(barrier, inc=1, device_id=near_device(k, j), device_id_type=MESH)
+    for h in range(1, z_count):
+        pl.semaphore_signal(barrier, inc=1, device_id=far_device(h), device_id_type=MESH)
+    pl.semaphore_wait(barrier, members - 1 + z_count - 1)
+
+    copies = []
+    for at, (k, j) in enumerate(others):
+        copy = pltpu.make_async_remote_copy(
+            part_ref.at[block(*place(k, j))], near.at[at], near_send.at[at], near_recv.at[at],
+            device_id=near_device(k, j), device_id_type=MESH,
+        )
+        copy.start()
+        copies.append(copy)
+    total = part_ref[block(g, b), :]
+    for at, copy in enumerate(copies):
+        copy.wait_recv()
+        total = total + near[at]
+    far[z] = total
+    for h in range(1, z_count):
+        copy = pltpu.make_async_remote_copy(
+            far.at[z], far.at[z], far_send.at[h - 1], far_recv.at[h - 1],
+            device_id=far_device(h), device_id_type=MESH,
+        )
+        copy.start()
+        copies.append(copy)
+    for copy in copies[len(others):]:
+        copy.wait_recv()
+    total = far[0]
+    for h in range(1, z_count):
+        total = total + far[h]
+    own = block(g, b)
+    whole[own, :] = total * scale
+    last = []
+    for at, (k, j) in enumerate(others):
+        copy = pltpu.make_async_remote_copy(
+            whole.at[own], whole.at[own], all_send.at[at], all_recv.at[at],
+            device_id=near_device(k, j), device_id_type=MESH,
+        )
+        copy.start()
+        last.append(copy)
+    for copy in last:
+        copy.wait_recv()
+    out_ref[...] = whole[...]
+    for copy in copies + last:
+        copy.wait_send()
+
+
+def sum_everywhere(part, bands, doms, scale):
+    size = part.shape[0]
+    others = GROUP * bands - 1
+    z_count = doms // GROUP
+    rows = size // (GROUP * bands)
+    dma = pltpu.SemaphoreType.DMA
+    vmem = pl.BlockSpec(memory_space=pltpu.VMEM)
+    far = max(z_count - 1, 1)
+    return pl.pallas_call(
+        functools.partial(sum_kernel, bands, doms, scale),
+        out_shape=jax.ShapeDtypeStruct(part.shape, jnp.float32),
+        in_specs=[vmem],
+        out_specs=vmem,
+        scratch_shapes=[
+            pltpu.VMEM((others, rows, size), jnp.float32),
+            pltpu.VMEM((z_count, rows, size), jnp.float32),
+            pltpu.VMEM(part.shape, jnp.float32),
+            dma((others,)), dma((others,)), dma((far,)), dma((far,)), dma((others,)), dma((others,)),
+        ],
+        compiler_params=pltpu.CompilerParams(
+            collective_id=1, has_side_effects=True, vmem_limit_bytes=16 * 2**20
+        ),
+        name="sum_everywhere",
+    )(part)
+
+
+BLOCK = 128
+
+
+def inverse_factor_kernel(gram_ref, out_ref, full, diag):
+    size = gram_ref.shape[0]
+    exact = lax.Precision.HIGHEST
+    full[...] = gram_ref[...]
+    row_id = lax.broadcasted_iota(jnp.int32, (BLOCK, BLOCK), 0)
+    lane_id = lax.broadcasted_iota(jnp.int32, (BLOCK, BLOCK), 1)
+    one_row = lax.broadcasted_iota(jnp.int32, (1, BLOCK), 1)
+    for first in range(0, size, BLOCK):
+        here, after = slice(first, first + BLOCK), first + BLOCK
+        diag[...] = full[here, here]
+
+        def eliminate(j, _):
+            held = diag[...]
+            row = diag[pl.ds(j, 1), :]
+            pivot = jnp.sum(jnp.where(one_row == j, row, 0.0), axis=1, keepdims=True)
+            column = jnp.sum(jnp.where(lane_id == j, held, 0.0), axis=1, keepdims=True)
+            root = lax.rsqrt(pivot)
+            root = root * (1.5 - 0.5 * pivot * root * root)
+            scaled = jnp.where(one_row == j, 1.0, row) * root
+            rest = jnp.where(lane_id == j, 0.0, held) - (column * root) * scaled
+            diag[...] = jnp.where(row_id > j, rest, held)
+            diag[pl.ds(j, 1), :] = scaled
+            return 0
+
+        lax.fori_loop(0, BLOCK, eliminate, 0)
+        inverse = jnp.where(row_id >= lane_id, diag[...], 0.0)
+        if first:
+            full[here, :first] = jnp.dot(
+                inverse, full[here, :first], precision=exact, preferred_element_type=jnp.float32
+            )
+        full[here, here] = inverse
+        if after < size:
+            upper = jnp.dot(
+                inverse, full[here, after:], precision=exact, preferred_element_type=jnp.float32
+            )
+            full[here, after:] = upper
+            full[after:, here] = jnp.zeros((size - after, BLOCK), jnp.float32)
+            full[after:, :] -= lax.dot_general(
+                upper, full[here, :], (((0,), (0,)), ((), ())),
+                precision=exact, preferred_element_type=jnp.float32,
+            )
+    row_all = lax.broadcasted_iota(jnp.int32, (size, size), 0)
+    lane_all = lax.broadcasted_iota(jnp.int32, (size, size), 1)
+    out_ref[...] = jnp.where(row_all >= lane_all, full[...], 0.0).astype(jnp.bfloat16)
+
+
 def rotation_from(gram):
-    factor = jnp.linalg.cholesky(gram)
-    identity = jnp.eye(gram.shape[0], dtype=jnp.float32)
-    inverse_factor = lax.linalg.triangular_solve(factor, identity, left_side=True, lower=True)
-    return inverse_factor.astype(jnp.bfloat16)
+    size = gram.shape[0]
+    vmem = pl.BlockSpec(memory_space=pltpu.VMEM)
+    return pl.pallas_call(
+        inverse_factor_kernel,
+        out_shape=jax.ShapeDtypeStruct(gram.shape, jnp.bfloat16),
+        in_specs=[vmem],
+        out_specs=vmem,
+        scratch_shapes=[
+            pltpu.VMEM(gram.shape, jnp.float32), pltpu.VMEM((BLOCK, BLOCK), jnp.float32)
+        ],
+        compiler_params=pltpu.CompilerParams(vmem_limit_bytes=16 * 2**20),
+        cost_estimate=pl.CostEstimate(
+            flops=40 * size**3, bytes_accessed=100 * 2**20, transcendentals=0
+        ),
+        name="inverse_factor",
+    )(gram)
 
 
 def local(bands, doms, orbitals, potential):
@@ -343,7 +502,7 @@
     for j in range(1, bands):
         ring = [((i + j) % bands, i) for i in range(bands)]
         pieces.append(lax.ppermute(held, "band", ring))
-    gram = lax.psum(part, ("band", "dom")) / total_cells
+    gram = sum_everywhere(part, bands, doms, 1.0 / total_cells)
     rotation = rotation_from(gram)
     b = lax.axis_index("band")
     own_rows = lax.dynamic_slice_in_dim(rotation, b * orbs, orbs, 0)

time: 423 us -> 319 us (0.75); the launches traced: 415 us -> 319 us
  Pallas kernels: 131 us -> 317 us
  waiting for transfers between devices: 125 us -> 0.01 us
  other arithmetic: 123 us -> 0.01 us
  between operations: 16.5 us -> 0.06 us
  local copies, waits for them, and re-layouts: 13.5 us -> 1.26 us
  matrix products: 5.81 us -> 0 us
    pallas_call x0 -> x2, Pallas kernels: none -> 187 us  [the longest x1 129 us: sum_everywhere(): pl.pallas_call(functools.partial(sum_kernel, bands, doms, scale), out_sha...]
    psum x1 -> x0, waiting for transfers between devices: 125 us -> none  [local(): gram = lax.psum(part, ('band', 'dom')) / total_cells]
    another operation x18 -> x0, other arithmetic: 120 us -> none  [the longest x14 78.7 us: rotation_from(): factor = jnp.linalg.cholesky(gram)]
    another operation x17 -> x0, local copies, waits for them, and re-layouts: 10.6 us -> none
    another operation x13 -> x0, matrix products: 5.81 us -> none  [the longest x7 3.94 us: rotation_from(): lax.linalg.triangular_solve(factor, identity, left_side=True, lower=True)]
  transfers between devices with their start and end apart: 2 -> 1, of which waited for: 1 -> 0; matrix products, arithmetic and copies ran while one was open for 34% -> 0% of each run, Pallas kernels for 0% -> 59%
where the time goes in v2:
time: 319 us
  Pallas kernels  317 us (99%)
    pallas_call x1, Pallas kernels, sum_everywhere(): pl.pallas_call(functools.partial(sum_kernel, bands, doms, scale), out_sha...  129 us
    pallas_call x1, Pallas kernels, filter_and_gram(): pl.pallas_call(functools.partial(filter_kernel, bands, doms), out_shape=(...  114 us
    pallas_call x1, Pallas kernels, rotation_from(): pl.pallas_call(inverse_factor_kernel, out_shape=jax.ShapeDtypeStruct(gram...  57.9 us
    pallas_call x1, Pallas kernels, rotate(): pl.pallas_call(rotate_kernel, out_shape=jax.ShapeDtypeStruct((orbs, all_r...  15.9 us
  transfers between devices with their start and end apart: 1, of which 0 were waited for; matrix products, arithmetic and copies ran while one was open for 0% of the time, Pallas kernels for 59%

profile of v2, /device:TPU:9, one launch (start us, length us, event | category | flops | bytes accessed | tf_op | source)
XLA Modules:
  0.0 318.9 jit_solution(3658940226317614873)
XLA Ops:
  0.0 114.1 %filter_and_gram.1 = (f32[512,512]{1,0:T(8,128)}, bf16[32,32,16,128]{3,2,1,0:T(8,128)(2,1)}) custom-call(bf16[256,2,32,128]{3,2,1,0:T(8,128)(2,1)} %orb_ref.1, f32[2,32,128]{2,1,0:T(8,128)} %pot_ref.1, bf16[256,256]{1,0:T(8,128)(2,1)} %constant.32.clone.ty_ref, bf16[128,128]{1,0:T(8,128)(2,1)} %constant.33.clone.tz_ref), custom_call_target="tpu_custom_call" | custom-call | tf_op jit(solution)/shard_map/filter_and_gram/pallas_call | solution.py:261
  114.1 0.6 collective-permute-start
  114.8 0.0 copy-start.1
  114.8 1.2 copy-done.1
  116.0 128.9 %sum_everywhere.1.gram_ref = f32[512,512]{1,0:T(8,128)S(1)} custom-call(f32[512,512]{1,0:T(8,128)S(1)} %copy-done.1), custom_call_target="tpu_custom_call" | custom-call | tf_op jit(solution)/shard_map/sum_everywhere/pallas_call | solution.py:410
  245.0 0.0 copy-start
  245.0 57.9 %inverse_factor.1 = bf16[512,512]{1,0:T(8,128)(2,1)S(1)} custom-call(f32[512,512]{1,0:T(8,128)S(1)} %sum_everywhere.1.gram_ref), custom_call_target="tpu_custom_call" | custom-call | flops 5368709120 | bytes 104857600 | tf_op jit(solution)/shard_map/inverse_factor/pallas_call | solution.py:480
  302.9 0.0 collective-permute-done.refs_1_
  302.9 0.0 copy-done
  302.9 15.9 %rotate.1 = bf16[256,64,128]{2,1,0:T(8,128)(2,1)} custom-call(bf16[256,512]{1,0:T(8,128)(2,1)S(1)} %constant_dynamic-slice_fusion.own_ref, bf16[32,32,16,128]{3,2,1,0:T(8,128)(2,1)S(1)} %copy-done, bf16[32,32,16,128]{3,2,1,0:T(8,128)(2,1)} %collective-permute-done.refs_1_, s32[2]{0:T(128)S(1)} %fusion.refs_2_), custom_call_target="tpu_custom_call" | custom-call | tf_op jit(solution)/shard_map/rotate/pallas_call | solution.py:319
  (2 shorter events, 0.0 us)
Async XLA Ops:
  114.1 188.8 %collective-permute-start = (bf16[32,32,16,128]{3,2,1,0:T(8,128)(2,1)}, bf16[32,32,16,128]{3,2,1,0:T(8,128)(2,1)}, u32[]{:S(2)}, u32[]{:S(2)}) collective-permute-start(bf16[32,32,16,128]{3,2,1,0:T(8,128)(2,1)} %get-tuple-element.8.refs_0_), channel_id=1, source_target_pairs={{16,0},{0,16},{17,1},{1,17},{18,2},{2,18},{19,3},{3,19},{20,4},{4,... | collective-permute-start | bytes 12582920 | tf_op jit(solution)/shard_map/ppermute | solution.py:504
  114.8 1.2 copy-start.1
  245.0 58.0 %copy-start = (bf16[32,32,16,128]{3,2,1,0:T(8,128)(2,1)S(1)}, bf16[32,32,16,128]{3,2,1,0:T(8,128)(2,1)}, u32[]{:S(2)}) copy-start(bf16[32,32,16,128]{3,2,1,0:T(8,128)(2,1)} %get-tuple-element.8.refs_0_) | copy-start | bytes 12582916

commit v3 on v2

--- a/solution.py
+++ b/solution.py
@@ -21,7 +21,7 @@
 
 
 def filter_kernel(
-    bands, doms, orb_ref, pot_ref, ty_ref, tz_ref, gram_ref, held_ref,
+    bands, doms, orb_ref, pot_ref, ty_ref, tz_ref, gram_ref, held_ref, kept_ref,
     f0, f1, f2, pot, wide, sent, held,
     in_send, in_recv, pot_send, pot_recv, halo_send, halo_recv, out_send, out_recv, own_sem,
 ):
@@ -173,10 +173,13 @@
 
             lax.fori_loop(0, slab, body, 0)
 
-    own_out, out_copies = [], []
+    own_out, out_copies, kept = [], [], []
 
     def send_out(c):
         landing = held.at[(b * GROUP + g) * chunks + c]
+        copy = pltpu.make_async_copy(sent.at[c], kept_ref.at[c], own_sem.at[2 * chunks + 2 + c])
+        copy.start()
+        kept.append(copy)
         for k in range(GROUP):
             for j in range(bands):
                 row = lax.rem(g + k, GROUP) * rows_dev + lax.rem(b + j, bands) * rows_part
@@ -244,6 +247,8 @@
             wait_halo_sent(s, c)
     for copy in out_copies:
         copy.wait_send()
+    for copy in kept:
+        copy.wait()
     keep.wait()
 
 
@@ -263,9 +268,10 @@
         out_shape=(
             jax.ShapeDtypeStruct((bands * orbs, bands * orbs), jnp.float32),
             jax.ShapeDtypeStruct(held, jnp.bfloat16),
+            jax.ShapeDtypeStruct((chunks, slab * ny, CHUNK, nz), jnp.bfloat16),
         ),
         in_specs=[hbm, vmem, vmem, vmem],
-        out_specs=(vmem, hbm),
+        out_specs=(vmem, hbm, hbm),
         scratch_shapes=[
             field, field, field,
             pltpu.VMEM((slab, ny, nz), jnp.float32),
@@ -276,7 +282,7 @@
             dma((GROUP - 1,)), dma((GROUP - 1,)),
             dma((3, chunks, 2)), dma((3, chunks, 2)),
             dma((chunks, others)), dma((chunks, others)),
-            dma((2 * chunks + 2,)),
+            dma((3 * chunks + 2,)),
         ],
         compiler_params=pltpu.CompilerParams(
             collective_id=0, has_side_effects=True, vmem_limit_bytes=56 * 2**20
@@ -285,46 +291,52 @@
     )(orbitals, potential, band_matrix(8, ny), band_matrix(1, nz))
 
 
-def rotate_kernel(own_ref, *refs):
-    pieces, (first_ref, out_ref, wide) = refs[:-3], refs[-3:]
-    count, rows, chunk, nz = pieces[0].shape
+def rotate_kernel(counts, first_ref, *refs):
+    refs, (out_ref, wide) = refs[:-2], refs[-2:]
     orbs, all_rows = out_ref.shape[0], out_ref.shape[1]
-    for j, piece in enumerate(pieces):
-        start = first_ref[j]
-
-        def body(i, _, piece=piece, start=start):
-            x = jnp.concatenate(
-                [piece[:, 2 * i + h].reshape(count * chunk, nz) for h in range(2)], axis=1
-            )
-            y = jnp.dot(own_ref[...], x, preferred_element_type=jnp.float32)
+    taken = 0
+    for at, count in enumerate(counts):
+        weight, parts = refs[taken], refs[taken + 1 : taken + 1 + count]
+        taken += 1 + count
+        rows, chunk, nz = parts[0].shape[1:]
+        start = first_ref[at]
+
+        def body(i, _, weight=weight, parts=parts, start=start, chunk=chunk, nz=nz):
+            def orbitals_at(row):
+                return jnp.concatenate(
+                    [part[:, row].reshape(part.shape[0] * chunk, nz) for part in parts], axis=0
+                )
+
+            x = jnp.concatenate([orbitals_at(2 * i), orbitals_at(2 * i + 1)], axis=1)
+            y = jnp.dot(weight[...], x, preferred_element_type=jnp.float32)
             for h in range(2):
-                at = pl.ds(start + 2 * i + h, orbs, stride=all_rows)
-                wide[at, :] = y[:, h * nz : (h + 1) * nz]
+                wide[pl.ds(start + 2 * i + h, orbs, stride=all_rows), :] = y[:, h * nz : (h + 1) * nz]
             return 0
 
         lax.fori_loop(0, rows // 2, body, 0)
 
     def narrow(i, _):
         part = wide[pl.ds(pl.multiple_of(i * 8 * all_rows, 8 * all_rows), 8 * all_rows), :]
-        out_ref[pl.ds(i * 8, 8)] = part.reshape(8, all_rows, nz).astype(jnp.bfloat16)
+        out_ref[pl.ds(i * 8, 8)] = part.reshape(8, all_rows, -1).astype(jnp.bfloat16)
         return 0
 
     lax.fori_loop(0, orbs // 8, narrow, 0)
 
 
-def rotate(own_rows, pieces, firsts, all_rows):
-    orbs = own_rows.shape[0]
-    nz = pieces[0].shape[3]
+def rotate(pieces, firsts, all_rows):
+    orbs = pieces[0][0].shape[0]
+    nz = pieces[0][1].shape[3]
     vmem = pl.BlockSpec(memory_space=pltpu.VMEM)
+    operands = [array for piece in pieces for array in piece]
     return pl.pallas_call(
-        rotate_kernel,
+        functools.partial(rotate_kernel, [len(piece) - 1 for piece in pieces]),
         out_shape=jax.ShapeDtypeStruct((orbs, all_rows, nz), jnp.bfloat16),
-        in_specs=[vmem] * (1 + len(pieces)) + [pl.BlockSpec(memory_space=pltpu.SMEM)],
+        in_specs=[pl.BlockSpec(memory_space=pltpu.SMEM)] + [vmem] * len(operands),
         out_specs=vmem,
         scratch_shapes=[pltpu.VMEM((orbs * all_rows, nz), jnp.float32)],
         compiler_params=pltpu.CompilerParams(vmem_limit_bytes=48 * 2**20),
         name="rotate",
-    )(own_rows, *pieces, firsts)
+    )(firsts, *operands)
 
 
 def sum_kernel(bands, doms, scale, part_ref, out_ref, near, far, whole, *sems):
@@ -426,6 +438,52 @@
 
 
 BLOCK = 128
+PIVOTS = 4
+
+
+def eliminate(diag, low, i, _):
+    first = low + i * PIVOTS
+    held = diag[low:, :]
+    row_id = lax.broadcasted_iota(jnp.int32, held.shape, 0) + low
+    lane_id = lax.broadcasted_iota(jnp.int32, held.shape, 1)
+    one_row = lax.broadcasted_iota(jnp.int32, (1, BLOCK), 1)
+    rows = [diag[pl.ds(first + p, 1), :] for p in range(PIVOTS)]
+
+    def pick(p, q):
+        return jnp.sum(jnp.where(one_row == first + q, rows[p], 0.0), axis=1, keepdims=True)
+
+    corner = [[pick(p, q) if q >= p else None for q in range(PIVOTS)] for p in range(PIVOTS)]
+    columns = [
+        jnp.sum(jnp.where(lane_id == first + p, held, 0.0), axis=1, keepdims=True)
+        for p in range(PIVOTS)
+    ]
+    roots, lower = [], [[None] * PIVOTS for _ in range(PIVOTS)]
+    for p in range(PIVOTS):
+        pivot = corner[p][p]
+        root = lax.rsqrt(pivot)
+        root = root * (1.5 - 0.5 * pivot * root * root)
+        roots.append(root)
+        for q in range(p + 1, PIVOTS):
+            lower[q][p] = corner[p][q] * root
+        for q in range(p + 1, PIVOTS):
+            for t in range(q, PIVOTS):
+                corner[q][t] = corner[q][t] - lower[q][p] * lower[t][p]
+    inside = (one_row >= first) & (one_row < first + PIVOTS)
+    rest = jnp.where((lane_id >= first) & (lane_id < first + PIVOTS), 0.0, held)
+    scaled, factors = [], []
+    for p in range(PIVOTS):
+        row = jnp.where(one_row == first + p, 1.0, jnp.where(inside, 0.0, rows[p]))
+        column = columns[p]
+        for t in range(p):
+            row = row - lower[p][t] * scaled[t]
+            column = column - factors[t] * lower[p][t]
+        scaled.append(row * roots[p])
+        factors.append(column * roots[p])
+        rest = rest - factors[p] * scaled[p]
+    diag[low:, :] = jnp.where(row_id >= first + PIVOTS, rest, held)
+    for p in range(PIVOTS):
+        diag[pl.ds(first + p, 1), :] = scaled[p]
+    return 0
 
 
 def inverse_factor_kernel(gram_ref, out_ref, full, diag):
@@ -434,25 +492,13 @@
     full[...] = gram_ref[...]
     row_id = lax.broadcasted_iota(jnp.int32, (BLOCK, BLOCK), 0)
     lane_id = lax.broadcasted_iota(jnp.int32, (BLOCK, BLOCK), 1)
-    one_row = lax.broadcasted_iota(jnp.int32, (1, BLOCK), 1)
     for first in range(0, size, BLOCK):
         here, after = slice(first, first + BLOCK), first + BLOCK
         diag[...] = full[here, here]
 
-        def eliminate(j, _):
-            held = diag[...]
-            row = diag[pl.ds(j, 1), :]
-            pivot = jnp.sum(jnp.where(one_row == j, row, 0.0), axis=1, keepdims=True)
-            column = jnp.sum(jnp.where(lane_id == j, held, 0.0), axis=1, keepdims=True)
-            root = lax.rsqrt(pivot)
-            root = root * (1.5 - 0.5 * pivot * root * root)
-            scaled = jnp.where(one_row == j, 1.0, row) * root
-            rest = jnp.where(lane_id == j, 0.0, held) - (column * root) * scaled
-            diag[...] = jnp.where(row_id > j, rest, held)
-            diag[pl.ds(j, 1), :] = scaled
-            return 0
-
-        lax.fori_loop(0, BLOCK, eliminate, 0)
+        for low in range(0, BLOCK, BLOCK // 4):
+            eliminate_from = functools.partial(eliminate, diag, low)
+            lax.fori_loop(0, BLOCK // 4 // PIVOTS, eliminate_from, 0)
         inverse = jnp.where(row_id >= lane_id, diag[...], 0.0)
         if first:
             full[here, :first] = jnp.dot(
@@ -497,17 +543,40 @@
     orbs, planes, ny, nz = orbitals.shape
     all_rows = planes * ny
     total_cells = all_rows * nz * doms
-    part, held = filter_and_gram(orbitals, potential, bands, doms)
-    pieces = [held]
-    for j in range(1, bands):
-        ring = [((i + j) % bands, i) for i in range(bands)]
-        pieces.append(lax.ppermute(held, "band", ring))
+    part, held, kept = filter_and_gram(orbitals, potential, bands, doms)
     gram = sum_everywhere(part, bands, doms, 1.0 / total_cells)
+    gram, held, kept = lax.optimization_barrier((gram, held, kept))
+    b, d = lax.axis_index("band"), lax.axis_index("dom")
+    rows_part = all_rows // bands
+    if bands == 2:
+        g = d % GROUP
+        share = orbs // GROUP
+        count = orbs // CHUNK
+        partner = lax.dynamic_slice_in_dim(held, b * count, count, 0)
+        partner = lax.ppermute(partner, "band", [(0, 1), (1, 0)])
+        near = []
+        for k in range(GROUP):
+            row = (g + k) % GROUP * all_rows + (1 - b) * rows_part
+            piece = lax.dynamic_slice_in_dim(kept, row, rows_part, 1)
+            if k:
+                ring = [(i, i // GROUP * GROUP + (i + k) % GROUP) for i in range(doms)]
+                piece = lax.ppermute(piece, "dom", ring)
+            near.append(piece)
+    else:
+        rings = [[((i + j) % bands, i) for i in range(bands)] for j in range(1, bands)]
+        others = [lax.ppermute(held, "band", ring) for ring in rings]
     rotation = rotation_from(gram)
-    b = lax.axis_index("band")
     own_rows = lax.dynamic_slice_in_dim(rotation, b * orbs, orbs, 0)
-    firsts = (b + jnp.arange(bands, dtype=jnp.int32)) % bands * (all_rows // bands)
-    result = rotate(own_rows, pieces, firsts.astype(jnp.int32), all_rows)
+    pieces = [[own_rows, held]]
+    if bands == 2:
+        starts = [b * orbs + (g - k) % GROUP * share for k in range(GROUP)]
+        columns = [lax.dynamic_slice_in_dim(own_rows, start, share, 1) for start in starts]
+        columns.append(lax.dynamic_slice_in_dim(own_rows, (1 - b) * orbs, orbs, 1))
+        pieces.append([jnp.concatenate(columns, axis=1), *near, partner])
+    else:
+        pieces += [[own_rows, other] for other in others]
+    firsts = (b + jnp.arange(bands, dtype=jnp.int32)) % bands * rows_part
+    result = rotate(pieces, firsts.astype(jnp.int32), all_rows)
     return result.reshape(orbitals.shape)
 
 

time: 319 us -> 223 us (0.70)
  Pallas kernels: 317 us -> 192 us
  waiting for transfers between devices: 0.01 us -> 14.8 us
  local copies, waits for them, and re-layouts: 1.26 us -> 11.8 us
  starting transfers between devices: 0.65 us -> 4.23 us
    pallas_call x1, Pallas kernels: 129 us -> 39.3 us  [sum_everywhere(): pl.pallas_call(functools.partial(sum_kernel, bands, doms, scale), out_sha...]
    pallas_call x1, Pallas kernels: 57.9 us -> 22.2 us  [rotation_from(): pl.pallas_call(inverse_factor_kernel, out_shape=jax.ShapeDtypeStruct(gram...]
    ppermute x1 -> x4, waiting for transfers between devices: 0.01 us -> 14.8 us  [the longest x1 14.8 us: local(): partner = lax.ppermute(partner, 'band', [(0, 1), (1, 0)])]
    dynamic_slice x0 -> x4, local copies, waits for them, and re-layouts: none -> 7.21 us  [the longest x1 3.36 us: local(): partner = lax.dynamic_slice_in_dim(held, b * count, count, 0)]
    ppermute x1 -> x4, starting transfers between devices: 0.65 us -> 4.23 us  [the longest x3 3.27 us: local(): piece = lax.ppermute(piece, 'dom', ring)]
  transfers between devices with their start and end apart: 1 -> 4, of which waited for: 0 -> 1; matrix products, arithmetic and copies ran while one was open for 0% -> 2% of each run, Pallas kernels for 59% -> 10%
where the time goes in v3:
time: 223 us
  Pallas kernels  192 us (86%)
  waiting for transfers between devices  14.8 us (7%)
  local copies, waits for them, and re-layouts  11.8 us (5%)
  starting transfers between devices  4.23 us (2%)
    pallas_call x1, Pallas kernels, filter_and_gram(): pl.pallas_call(functools.partial(filter_kernel, bands, doms), out_shape=(...  114 us
    pallas_call x1, Pallas kernels, sum_everywhere(): pl.pallas_call(functools.partial(sum_kernel, bands, doms, scale), out_sha...  39.3 us
    pallas_call x1, Pallas kernels, rotation_from(): pl.pallas_call(inverse_factor_kernel, out_shape=jax.ShapeDtypeStruct(gram...  22.2 us
    pallas_call x1, Pallas kernels, rotate(): pl.pallas_call(functools.partial(rotate_kernel, [len(piece) - 1 for piece...  16.4 us
    ppermute x1, waiting for transfers between devices, local(): partner = lax.ppermute(partner, 'band', [(0, 1), (1, 0)])  14.8 us
  transfers between devices with their start and end apart: 4, of which 1 were waited for; matrix products, arithmetic and copies ran while one was open for 2% of the time, Pallas kernels for 10%

profile of v3, /device:TPU:9, one launch (start us, length us, event | category | flops | bytes accessed | tf_op | source)
XLA Modules:
  0.0 223.1 jit_solution(9275159300466760864)
XLA Ops:
  0.0 114.2 %filter_and_gram.1 = (f32[512,512]{1,0:T(8,128)}, bf16[32,32,16,128]{3,2,1,0:T(8,128)(2,1)}, bf16[4,256,16,128]{3,2,1,0:T(8,128)(2,1)}) custom-call(bf16[256,2,32,128]{3,2,1,0:T(8,128)(2,1)} %orb_ref.1, f32[2,32,128]{2,1,0:T(8,128)} %pot_ref.1, bf16[256,256]{1,0:T(8,128)(2,1)} %constant.141.clone.ty_ref, bf16[128,128]{1,0:T(8,128)(2,1)} %constant.142.clone.tz_ref), custom_call_target="tpu_custom_call" | custom-call | tf_op jit(solution)/shard_map/filter_and_gram/pallas_call | solution.py:266
  114.2 0.0 copy-start.2
  114.2 1.2 copy-done.2
  115.4 39.3 %sum_everywhere.1.gram_ref = f32[512,512]{1,0:T(8,128)S(1)} custom-call(f32[512,512]{1,0:T(8,128)S(1)} %copy-done.2), custom_call_target="tpu_custom_call" | custom-call | tf_op jit(solution)/shard_map/sum_everywhere/pallas_call | solution.py:422
  154.8 0.0 copy-start
  154.8 1.0 copy-done
  155.8 3.4 %constant_dynamic-slice_fusion = bf16[16,32,16,128]{3,2,1,0:T(8,128)(2,1)} fusion(bf16[32,32,16,128]{3,2,1,0:T(8,128)(2,1)} %get-tuple-element.15.refs_1_, s32[]{:T(128)S(6)} %select_n.113), kind=kLoop, calls=%fused_computation.3 | loop fusion | bytes 4194308 | tf_op jit(solution)/shard_map/dynamic_slice | solution.py:555
  159.2 1.0 collective-permute-start.3
  160.1 2.8 %constant_dynamic-slice_fusion.1 = (bf16[4,32,16,128]{3,2,1,0:T(8,128)(2,1)}, bf16[4,32,16,128]{3,2,1,0:T(8,128)(2,1)}, bf16[4,32,16,128]{3,2,1,0:T(8,128)(2,1)}, bf16[4,32,16,128]{3,2,1,0:T(8,128)(2,1)S(1)}) fusion(bf16[4,256,16,128]{3,2,1,0:T(8,128)(2,1)} %get-tuple-element.16, s32[]{:T(128)S(6)} %select_n.112, s32[]{:T(128)S(6)} %select_n.110, ...), kind=kLoop, calls=%fused_computation.4 | loop fusion | bytes 4194320 | tf_op jit(solution)/shard_map/dynamic_slice | solution.py:560
  163.0 1.0 collective-permute-start.2
  163.9 0.3 collective-permute-start.1
  164.2 2.0 collective-permute-start
  166.2 0.0 copy-start.1
  166.2 1.2 copy-done.1
  167.5 22.2 %inverse_factor.1 = bf16[512,512]{1,0:T(8,128)(2,1)S(1)} custom-call(f32[512,512]{1,0:T(8,128)S(1)} %copy-done.1), custom_call_target="tpu_custom_call" | custom-call | flops 5368709120 | bytes 104857600 | tf_op jit(solution)/shard_map/inverse_factor/pallas_call | solution.py:526
  189.8 0.1 dynamic_slice.38
  189.9 0.9 fusion.2
  190.8 1.1 concatenate.3.refs_2_
  191.9 0.0 collective-permute-done.2.refs_6_
  191.9 0.0 collective-permute-done.1.refs_5_
  191.9 0.0 collective-permute-done.refs_4_
  191.9 14.8 %collective-permute-done.3.refs_7_ = bf16[16,32,16,128]{3,2,1,0:T(8,128)(2,1)S(1)} collective-permute-done((bf16[16,32,16,128]{3,2,1,0:T(8,128)(2,1)}, bf16[16,32,16,128]{3,2,1,0:T(8,128)(2,1)S(1)}, u32[]{:S(2)}, u32[]{:S(2)}) %collective-permute-start.3) | collective-permute-done | bytes 2097184 | tf_op jit(solution)/shard_map/ppermute | solution.py:556
  206.8 16.4 %rotate.1 = bf16[256,64,128]{2,1,0:T(8,128)(2,1)} custom-call(s32[2]{0:T(128)S(1)} %fusion.first_ref, bf16[256,512]{1,0:T(8,128)(2,1)S(1)} %constant_dynamic-slice_fusion.5.refs_0_, bf16[32,32,16,128]{3,2,1,0:T(8,128)(2,1)} %get-tuple-element.15.refs_1_, bf16[256,512]{1,0:T(8,128)(2,1)S(1)} %concatenate.3.refs_2_, ...), custom_call_target="tpu_custom_call" | custom-call | tf_op jit(solution)/shard_map/rotate/pallas_call | solution.py:331
  (2 shorter events, 0.0 us)
Async XLA Ops:
  114.2 1.2 copy-start.2
  154.8 1.1 copy-start
  159.2 47.6 %collective-permute-start.3 = (bf16[16,32,16,128]{3,2,1,0:T(8,128)(2,1)}, bf16[16,32,16,128]{3,2,1,0:T(8,128)(2,1)S(1)}, u32[]{:S(2)}, u32[]{:S(2)}) collective-permute-start(bf16[16,32,16,128]{3,2,1,0:T(8,128)(2,1)} %constant_dynamic-slice_fusion), channel_id=1, source_target_pairs={{0,16},{16,0},{1,17},{17,1},{2,18},{18,2},{3,19},{19,3},{4,20},{20... | collective-permute-start | bytes 6291464 | tf_op jit(solution)/shard_map/ppermute | solution.py:556
  163.0 29.0 %collective-permute-start.2 = (bf16[4,32,16,128]{3,2,1,0:T(8,128)(2,1)}, bf16[4,32,16,128]{3,2,1,0:T(8,128)(2,1)}, u32[]{:S(2)}, u32[]{:S(2)}) collective-permute-start(bf16[4,32,16,128]{3,2,1,0:T(8,128)(2,1)} %get-tuple-element.17), channel_id=1, source_target_pairs={{0,3},{1,0},{2,1},{3,2},{4,7},{5,4},{6,5},{7,6},{8,11},{9,8},{10,9... | collective-permute-start | bytes 1572872 | tf_op jit(solution)/shard_map/ppermute | solution.py:563
  163.9 28.0 %collective-permute-start.1 = (bf16[4,32,16,128]{3,2,1,0:T(8,128)(2,1)}, bf16[4,32,16,128]{3,2,1,0:T(8,128)(2,1)}, u32[]{:S(2)}, u32[]{:S(2)}) collective-permute-start(bf16[4,32,16,128]{3,2,1,0:T(8,128)(2,1)} %get-tuple-element.18), channel_id=1, source_target_pairs={{0,2},{1,3},{2,0},{3,1},{4,6},{5,7},{6,4},{7,5},{8,10},{9,11},{10,... | collective-permute-start | bytes 1572872 | tf_op jit(solution)/shard_map/ppermute | solution.py:563
  164.2 27.7 %collective-permute-start = (bf16[4,32,16,128]{3,2,1,0:T(8,128)(2,1)}, bf16[4,32,16,128]{3,2,1,0:T(8,128)(2,1)}, u32[]{:S(2)}, u32[]{:S(2)}) collective-permute-start(bf16[4,32,16,128]{3,2,1,0:T(8,128)(2,1)} %get-tuple-element.19), channel_id=1, source_target_pairs={{0,1},{1,2},{2,3},{3,0},{4,5},{5,6},{6,7},{7,4},{8,9},{9,10},{10,1... | collective-permute-start | bytes 1572872 | tf_op jit(solution)/shard_map/ppermute | solution.py:563
  166.2 1.2 copy-start.1

commit v4 on v3

--- a/solution.py
+++ b/solution.py
@@ -18,6 +18,14 @@
 def band_matrix(blocks, size):
     one = 16.0 * (np.eye(size, k=1) + np.eye(size, k=-1)) - np.eye(size, k=2) - np.eye(size, k=-2)
     return jnp.asarray(np.kron(np.eye(blocks), one), jnp.bfloat16)
+
+
+BLOCK = 128
+
+
+def lower_blocks(size):
+    count = size // BLOCK
+    return [(i, j) for i in range(count) for j in range(i + 1)]
 
 
 def filter_kernel(
@@ -232,7 +240,9 @@
         part = lax.dot_general(
             x, x, (((1,), (1,)), ((), ())), preferred_element_type=jnp.float32
         )
-        gram_ref[...] += part
+        for at, (i, j) in enumerate(lower_blocks(everyone)):
+            tile = part[i * BLOCK : (i + 1) * BLOCK, j * BLOCK : (j + 1) * BLOCK]
+            gram_ref[at * BLOCK : (at + 1) * BLOCK, :] += tile
         return 0
 
     gram_ref[...] = jnp.zeros(gram_ref.shape, jnp.float32)
@@ -266,7 +276,9 @@
     return pl.pallas_call(
         functools.partial(filter_kernel, bands, doms),
         out_shape=(
-            jax.ShapeDtypeStruct((bands * orbs, bands * orbs), jnp.float32),
+            jax.ShapeDtypeStruct(
+                (len(lower_blocks(bands * orbs)) * BLOCK, BLOCK), jnp.float32
+            ),
             jax.ShapeDtypeStruct(held, jnp.bfloat16),
             jax.ShapeDtypeStruct((chunks, slab * ny, CHUNK, nz), jnp.bfloat16),
         ),
@@ -291,9 +303,10 @@
     )(orbitals, potential, band_matrix(8, ny), band_matrix(1, nz))
 
 
-def rotate_kernel(counts, first_ref, *refs):
+def rotate_kernel(counts, early, first_ref, *refs):
     refs, (out_ref, wide) = refs[:-2], refs[-2:]
-    orbs, all_rows = out_ref.shape[0], out_ref.shape[1]
+    orbs = out_ref.shape[0]
+    all_rows = wide.shape[0] // orbs
     taken = 0
     for at, count in enumerate(counts):
         weight, parts = refs[taken], refs[taken + 1 : taken + 1 + count]
@@ -317,23 +330,36 @@
 
     def narrow(i, _):
         part = wide[pl.ds(pl.multiple_of(i * 8 * all_rows, 8 * all_rows), 8 * all_rows), :]
-        out_ref[pl.ds(i * 8, 8)] = part.reshape(8, all_rows, -1).astype(jnp.bfloat16)
+        part = part.reshape(8, all_rows, -1).astype(jnp.bfloat16)
+        if early:
+            some = pl.ds(i * 8, 8)
+            out_ref[some, pl.ds(pl.multiple_of(first_ref[len(counts)], all_rows), all_rows)] = part
+            at = pl.multiple_of(first_ref[len(counts) + 1], all_rows)
+            out_ref[some, pl.ds(at, all_rows)] = refs[-1][some]
+        else:
+            out_ref[pl.ds(i * 8, 8)] = part
         return 0
 
     lax.fori_loop(0, orbs // 8, narrow, 0)
 
 
-def rotate(pieces, firsts, all_rows):
+def rotate(pieces, firsts, all_rows, early=None):
     orbs = pieces[0][0].shape[0]
     nz = pieces[0][1].shape[3]
     vmem = pl.BlockSpec(memory_space=pltpu.VMEM)
     operands = [array for piece in pieces for array in piece]
+    made = all_rows
+    if early is not None:
+        operands.append(early)
+        made -= early.shape[1]
     return pl.pallas_call(
-        functools.partial(rotate_kernel, [len(piece) - 1 for piece in pieces]),
+        functools.partial(
+            rotate_kernel, [len(piece) - 1 for piece in pieces], early is not None
+        ),
         out_shape=jax.ShapeDtypeStruct((orbs, all_rows, nz), jnp.bfloat16),
         in_specs=[pl.BlockSpec(memory_space=pltpu.SMEM)] + [vmem] * len(operands),
         out_specs=vmem,
-        scratch_shapes=[pltpu.VMEM((orbs * all_rows, nz), jnp.float32)],
+        scratch_shapes=[pltpu.VMEM((orbs * made, nz), jnp.float32)],
         compiler_params=pltpu.CompilerParams(vmem_limit_bytes=48 * 2**20),
         name="rotate",
     )(firsts, *operands)
@@ -412,7 +438,7 @@
 
 
 def sum_everywhere(part, bands, doms, scale):
-    size = part.shape[0]
+    size, width = part.shape
     others = GROUP * bands - 1
     z_count = doms // GROUP
     rows = size // (GROUP * bands)
@@ -425,8 +451,8 @@
         in_specs=[vmem],
         out_specs=vmem,
         scratch_shapes=[
-            pltpu.VMEM((others, rows, size), jnp.float32),
-            pltpu.VMEM((z_count, rows, size), jnp.float32),
+            pltpu.VMEM((others, rows, width), jnp.float32),
+            pltpu.VMEM((z_count, rows, width), jnp.float32),
             pltpu.VMEM(part.shape, jnp.float32),
             dma((others,)), dma((others,)), dma((far,)), dma((far,)), dma((others,)), dma((others,)),
         ],
@@ -437,7 +463,6 @@
     )(part)
 
 
-BLOCK = 128
 PIVOTS = 4
 
 
@@ -487,9 +512,14 @@
 
 
 def inverse_factor_kernel(gram_ref, out_ref, full, diag):
-    size = gram_ref.shape[0]
+    size = full.shape[0]
     exact = lax.Precision.HIGHEST
-    full[...] = gram_ref[...]
+    for at, (i, j) in enumerate(lower_blocks(size)):
+        rows, lanes = slice(i * BLOCK, (i + 1) * BLOCK), slice(j * BLOCK, (j + 1) * BLOCK)
+        tile = gram_ref[at * BLOCK : (at + 1) * BLOCK, :]
+        full[rows, lanes] = tile
+        if i != j:
+            full[lanes, rows] = tile.T
     row_id = lax.broadcasted_iota(jnp.int32, (BLOCK, BLOCK), 0)
     lane_id = lax.broadcasted_iota(jnp.int32, (BLOCK, BLOCK), 1)
     for first in range(0, size, BLOCK):
@@ -520,16 +550,15 @@
     out_ref[...] = jnp.where(row_all >= lane_all, full[...], 0.0).astype(jnp.bfloat16)
 
 
-def rotation_from(gram):
-    size = gram.shape[0]
+def rotation_from(gram, size):
     vmem = pl.BlockSpec(memory_space=pltpu.VMEM)
     return pl.pallas_call(
         inverse_factor_kernel,
-        out_shape=jax.ShapeDtypeStruct(gram.shape, jnp.bfloat16),
+        out_shape=jax.ShapeDtypeStruct((size, size), jnp.bfloat16),
         in_specs=[vmem],
         out_specs=vmem,
         scratch_shapes=[
-            pltpu.VMEM(gram.shape, jnp.float32), pltpu.VMEM((BLOCK, BLOCK), jnp.float32)
+            pltpu.VMEM((size, size), jnp.float32), pltpu.VMEM((BLOCK, BLOCK), jnp.float32)
         ],
         compiler_params=pltpu.CompilerParams(vmem_limit_bytes=16 * 2**20),
         cost_estimate=pl.CostEstimate(
@@ -565,18 +594,21 @@
     else:
         rings = [[((i + j) % bands, i) for i in range(bands)] for j in range(1, bands)]
         others = [lax.ppermute(held, "band", ring) for ring in rings]
-    rotation = rotation_from(gram)
+    rotation = rotation_from(gram, bands * orbs)
     own_rows = lax.dynamic_slice_in_dim(rotation, b * orbs, orbs, 0)
     pieces = [[own_rows, held]]
     if bands == 2:
         starts = [b * orbs + (g - k) % GROUP * share for k in range(GROUP)]
         columns = [lax.dynamic_slice_in_dim(own_rows, start, share, 1) for start in starts]
         columns.append(lax.dynamic_slice_in_dim(own_rows, (1 - b) * orbs, orbs, 1))
-        pieces.append([jnp.concatenate(columns, axis=1), *near, partner])
+        early = rotate(pieces, jnp.zeros((1,), jnp.int32), rows_part)
+        pieces = [[jnp.concatenate(columns, axis=1), *near, partner]]
+        places = jnp.stack([jnp.zeros_like(b), (1 - b) * rows_part, b * rows_part])
+        result = rotate(pieces, places.astype(jnp.int32), all_rows, early)
     else:
         pieces += [[own_rows, other] for other in others]
-    firsts = (b + jnp.arange(bands, dtype=jnp.int32)) % bands * rows_part
-    result = rotate(pieces, firsts.astype(jnp.int32), all_rows)
+        firsts = (b + jnp.arange(bands, dtype=jnp.int32)) % bands * rows_part
+        result = rotate(pieces, firsts.astype(jnp.int32), all_rows)
     return result.reshape(orbitals.shape)
 
 

time: 223 us -> 205 us (0.919)
  Pallas kernels: 192 us -> 182 us
  waiting for transfers between devices: 14.8 us -> 8.05 us
    pallas_call x1, Pallas kernels: 39.3 us -> 27.9 us  [sum_everywhere(): pl.pallas_call(functools.partial(sum_kernel, bands, doms, scale), out_sha...]
    ppermute x1, waiting for transfers between devices: 14.8 us -> 8.04 us  [local(): partner = lax.ppermute(partner, 'band', [(0, 1), (1, 0)])]
    pallas_call x1 -> x2, Pallas kernels: 16.4 us -> 18.3 us  [rotate(): pl.pallas_call(functools.partial(rotate_kernel, [len(piece) - 1 for piece...]
  transfers between devices with their start and end apart: 4 -> 4, of which waited for: 1 -> 1; matrix products, arithmetic and copies ran while one was open for 2% -> 2% of each run, Pallas kernels for 10% -> 15%
where the time goes in v4:
time: 205 us
  Pallas kernels  182 us (89%)
  local copies, waits for them, and re-layouts  11 us (5%)
  waiting for transfers between devices  8.05 us (4%)
  starting transfers between devices  3.19 us (2%)
    pallas_call x1, Pallas kernels, filter_and_gram(): pl.pallas_call(functools.partial(filter_kernel, bands, doms), out_shape=(...  114 us
    pallas_call x1, Pallas kernels, sum_everywhere(): pl.pallas_call(functools.partial(sum_kernel, bands, doms, scale), out_sha...  27.9 us
    pallas_call x1, Pallas kernels, rotation_from(): pl.pallas_call(inverse_factor_kernel, out_shape=jax.ShapeDtypeStruct((siz...  22.3 us
    pallas_call x2, Pallas kernels, rotate(): pl.pallas_call(functools.partial(rotate_kernel, [len(piece) - 1 for piece...  18.3 us
    ppermute x1, waiting for transfers between devices, local(): partner = lax.ppermute(partner, 'band', [(0, 1), (1, 0)])  8.04 us
    unnamed x8, local copies, waits for them, and re-layouts  4.37 us
  transfers between devices with their start and end apart: 4, of which 1 were waited for; matrix products, arithmetic and copies ran while one was open for 2% of the time, Pallas kernels for 15%

profile of v4, /device:TPU:9, one launch (start us, length us, event | category | flops | bytes accessed | tf_op | source)
XLA Modules:
  0.0 205.0 jit_solution(12572255511507868751)
XLA Ops:
  0.0 114.0 %filter_and_gram.1 = (f32[1280,128]{1,0:T(8,128)}, bf16[32,32,16,128]{3,2,1,0:T(8,128)(2,1)}, bf16[4,256,16,128]{3,2,1,0:T(8,128)(2,1)}) custom-call(bf16[256,2,32,128]{3,2,1,0:T(8,128)(2,1)} %orb_ref.1, f32[2,32,128]{2,1,0:T(8,128)} %pot_ref.1, bf16[256,256]{1,0:T(8,128)(2,1)} %constant.131.clone.ty_ref, bf16[128,128]{1,0:T(8,128)(2,1)} %constant.132.clone.tz_ref), custom_call_target="tpu_custom_call" | custom-call | tf_op jit(solution)/shard_map/filter_and_gram/pallas_call | solution.py:276
  114.0 0.0 copy-start.3
  114.0 1.1 copy-done.3
  115.1 27.9 %sum_everywhere.1.gram_ref = f32[1280,128]{1,0:T(8,128)S(1)} custom-call(f32[1280,128]{1,0:T(8,128)S(1)} %copy-done.3), custom_call_target="tpu_custom_call" | custom-call | tf_op jit(solution)/shard_map/sum_everywhere/pallas_call | solution.py:448
  143.0 0.0 copy-start.1
  143.0 0.9 copy-done.1
  143.9 3.4 %constant_dynamic-slice_fusion.1 = bf16[16,32,16,128]{3,2,1,0:T(8,128)(2,1)} fusion(bf16[32,32,16,128]{3,2,1,0:T(8,128)(2,1)} %get-tuple-element.16.refs_1_, s32[]{:T(128)S(6)} %select_n.106), kind=kLoop, calls=%fused_computation.1 | loop fusion | bytes 4194308 | tf_op jit(solution)/shard_map/dynamic_slice | solution.py:584
  147.3 1.0 collective-permute-start.3
  148.3 2.8 %constant_dynamic-slice_fusion.2 = (bf16[4,32,16,128]{3,2,1,0:T(8,128)(2,1)}, bf16[4,32,16,128]{3,2,1,0:T(8,128)(2,1)}, bf16[4,32,16,128]{3,2,1,0:T(8,128)(2,1)}, bf16[4,32,16,128]{3,2,1,0:T(8,128)(2,1)S(1)}) fusion(bf16[4,256,16,128]{3,2,1,0:T(8,128)(2,1)} %get-tuple-element.15, s32[]{:T(128)S(6)} %select_n.105, s32[]{:T(128)S(6)} %select_n.103, ...), kind=kLoop, calls=%fused_computation.2 | loop fusion | bytes 4194320 | tf_op jit(solution)/shard_map/dynamic_slice | solution.py:589
  151.1 0.0 collective-permute-start
  151.1 2.1 %collective-permute-start.1 = (bf16[4,32,16,128]{3,2,1,0:T(8,128)(2,1)}, bf16[4,32,16,128]{3,2,1,0:T(8,128)(2,1)}, u32[]{:S(2)}, u32[]{:S(2)}) collective-permute-start(bf16[4,32,16,128]{3,2,1,0:T(8,128)(2,1)} %get-tuple-element.18), channel_id=1, source_target_pairs={{0,2},{1,3},{2,0},{3,1},{4,6},{5,7},{6,4},{7,5},{8,10},{9,11},{10,... | collective-permute-start | bytes 1572872 | tf_op jit(solution)/shard_map/ppermute | solution.py:592
  153.3 0.0 collective-permute-start.2
  153.3 0.0 copy-start.2
  153.3 1.1 copy-done.2
  154.4 22.3 %inverse_factor.1 = bf16[512,512]{1,0:T(8,128)(2,1)S(1)} custom-call(f32[1280,128]{1,0:T(8,128)S(1)} %copy-done.2), custom_call_target="tpu_custom_call" | custom-call | flops 5368709120 | bytes 104857600 | tf_op jit(solution)/shard_map/inverse_factor/pallas_call | solution.py:555
  176.8 0.1 dynamic_slice.37
  176.9 8.1 %rotate.2.refs_6_ = bf16[256,32,128]{2,1,0:T(8,128)(2,1)S(1)} custom-call(s32[1]{0:T(128)} %constant.113.clone.1.first_ref, bf16[256,512]{1,0:T(8,128)(2,1)S(1)} %constant_dynamic-slice_fusion.refs_0_, bf16[32,32,16,128]{3,2,1,0:T(8,128)(2,1)} %get-tuple-element.16.refs_1_), custom_call_target="tpu_custom_call" | custom-call | tf_op jit(solution)/shard_map/rotate/pallas_call | solution.py:355
  185.0 0.0 copy-start
  185.0 1.3 copy-done
  186.4 0.2 fusion
  186.6 0.1 concatenate.3.refs_0_
  186.7 0.1 pad_add_fusion.first_ref
  186.8 0.0 collective-permute-done.refs_2_
  186.8 0.0 collective-permute-done.1.refs_3_
  186.8 0.0 collective-permute-done.2.refs_4_
  186.8 8.0 %collective-permute-done.3.refs_5_ = bf16[16,32,16,128]{3,2,1,0:T(8,128)(2,1)S(1)} collective-permute-done((bf16[16,32,16,128]{3,2,1,0:T(8,128)(2,1)}, bf16[16,32,16,128]{3,2,1,0:T(8,128)(2,1)S(1)}, u32[]{:S(2)}, u32[]{:S(2)}) %collective-permute-start.3) | collective-permute-done | bytes 2097184 | tf_op jit(solution)/shard_map/ppermute | solution.py:585
  194.9 10.2 %rotate.3 = bf16[256,64,128]{2,1,0:T(8,128)(2,1)} custom-call(s32[3]{0:T(128)S(1)} %pad_add_fusion.first_ref, bf16[256,512]{1,0:T(8,128)(2,1)S(1)} %concatenate.3.refs_0_, bf16[4,32,16,128]{3,2,1,0:T(8,128)(2,1)S(1)} %get-tuple-element.20.refs_1_, bf16[4,32,16,128]{3,2,1,0:T(8,128)(2,1)} %collective-permute-done.refs_2_, ...), custom_call_target="tpu_custom_call" | custom-call | tf_op jit(solution)/shard_map/rotate/pallas_call | solution.py:355
  (1 shorter events, 0.0 us)
Async XLA Ops:
  114.0 1.1 copy-start.3
  143.0 0.9 copy-start.1
  147.3 47.6 %collective-permute-start.3 = (bf16[16,32,16,128]{3,2,1,0:T(8,128)(2,1)}, bf16[16,32,16,128]{3,2,1,0:T(8,128)(2,1)S(1)}, u32[]{:S(2)}, u32[]{:S(2)}) collective-permute-start(bf16[16,32,16,128]{3,2,1,0:T(8,128)(2,1)} %constant_dynamic-slice_fusion.1), channel_id=1, source_target_pairs={{0,16},{16,0},{1,17},{17,1},{2,18},{18,2},{3,19},{19,3},{4,20},{20... | collective-permute-start | bytes 6291464 | tf_op jit(solution)/shard_map/ppermute | solution.py:585
  151.1 35.7 %collective-permute-start = (bf16[4,32,16,128]{3,2,1,0:T(8,128)(2,1)}, bf16[4,32,16,128]{3,2,1,0:T(8,128)(2,1)}, u32[]{:S(2)}, u32[]{:S(2)}) collective-permute-start(bf16[4,32,16,128]{3,2,1,0:T(8,128)(2,1)} %get-tuple-element.19), channel_id=1, source_target_pairs={{0,1},{1,2},{2,3},{3,0},{4,5},{5,6},{6,7},{7,4},{8,9},{9,10},{10,1... | collective-permute-start | bytes 1572872 | tf_op jit(solution)/shard_map/ppermute | solution.py:592
  151.1 35.7 %collective-permute-start.1 = (bf16[4,32,16,128]{3,2,1,0:T(8,128)(2,1)}, bf16[4,32,16,128]{3,2,1,0:T(8,128)(2,1)}, u32[]{:S(2)}, u32[]{:S(2)}) collective-permute-start(bf16[4,32,16,128]{3,2,1,0:T(8,128)(2,1)} %get-tuple-element.18), channel_id=1, source_target_pairs={{0,2},{1,3},{2,0},{3,1},{4,6},{5,7},{6,4},{7,5},{8,10},{9,11},{10,... | collective-permute-start | bytes 1572872 | tf_op jit(solution)/shard_map/ppermute | solution.py:592
  153.3 33.5 %collective-permute-start.2 = (bf16[4,32,16,128]{3,2,1,0:T(8,128)(2,1)}, bf16[4,32,16,128]{3,2,1,0:T(8,128)(2,1)}, u32[]{:S(2)}, u32[]{:S(2)}) collective-permute-start(bf16[4,32,16,128]{3,2,1,0:T(8,128)(2,1)} %get-tuple-element.17), channel_id=1, source_target_pairs={{0,3},{1,0},{2,1},{3,2},{4,7},{5,4},{6,5},{7,6},{8,11},{9,8},{10,9... | collective-permute-start | bytes 1572872 | tf_op jit(solution)/shard_map/ppermute | solution.py:592
  153.3 1.1 copy-start.2
  185.0 1.3 copy-start
